TPU v7x, 256 devices: a whole 4x4x8 slice. The times are simulated.
256 devices in a mesh: inp: 8 (over z), wgt: 8 (over x_lo, y), out: 4 (over x_hi, core).
Axes of the slice: x: 4 (x_hi: 2, x_lo: 2; x = x_hi * 2 + x_lo), y: 4, z: 8, core: 2. Of those that a mesh axis runs over, the one named last changes fastest.
Arguments:
- tokens: bfloat16 [1024, 6144], P('out', ('wgt', 'inp')), may hold values from -6 to 6
- w_up: bfloat16 [6144, 24576], P(('wgt', 'out'), 'inp'), may hold values from -0.078125 to 0.078125
- w_down: bfloat16 [24576, 6144], P(('inp', 'out'), 'wgt'), may hold values from -0.0390625 to 0.0390625
- grad_out: bfloat16 [1024, 6144], P('out', ('wgt', 'inp')), may hold values from -6 to 6
Outputs:
- output: bfloat16 [1024, 6144], P('out', ('wgt', 'inp'))
- grad_tokens: bfloat16 [1024, 6144], P('out', ('wgt', 'inp'))
- grad_up: bfloat16 [6144, 24576], P(('wgt', 'out'), 'inp')
- grad_down: bfloat16 [24576, 6144], P(('inp', 'out'), 'wgt')
All inputs are finite; a program needn't handle non-finite values.
Results may differ from a plain program's by a relative error of at most 0.029.
Values may be sent and summed in bfloat16 or wider, within the bound.
No kernel may reach another device: no remote copies, remote signals or barrier semaphores. Data moves between devices by JAX's collectives and lax.ppermute only.
A program may use at most 64 MiB of HBM per device.

v0:
```python
import jax
import jax.numpy as jnp
from jax import lax
from jax.sharding import PartitionSpec as P

tanh_scale = 0.7978845608028654
cubic_weight = 0.044715


def gelu_value(hidden):
    tangent = jnp.tanh(tanh_scale * (hidden + cubic_weight * hidden * hidden * hidden))
    return 0.5 * hidden * (1.0 + tangent)


def gelu_slope(hidden):
    tangent = jnp.tanh(tanh_scale * (hidden + cubic_weight * hidden * hidden * hidden))
    return 0.5 * (1.0 + tangent) + 0.5 * hidden * (1.0 - tangent * tangent) * tanh_scale * (
        1.0 + 3.0 * cubic_weight * hidden * hidden
    )


def product(former, latter):
    return jnp.dot(former, latter, preferred_element_type=jnp.float32)


def against(former, latter):
    return lax.dot_general(
        former, latter, (((1,), (1,)), ((), ())), preferred_element_type=jnp.float32
    )


def across(former, latter):
    return lax.dot_general(
        former, latter, (((0,), (0,)), ((), ())), preferred_element_type=jnp.float32
    )


def share_features(partial_value):
    return lax.psum_scatter(
        partial_value.astype(jnp.bfloat16), "inp", scatter_dimension=1, tiled=True
    ).astype(jnp.float32)


def share_hidden(partial_value):
    return lax.psum_scatter(
        partial_value.astype(jnp.bfloat16), "wgt", scatter_dimension=1, tiled=True
    ).astype(jnp.float32)


def whole_hidden(portion):
    return lax.all_gather(portion, "wgt", axis=1, tiled=True)


def weight_grad(former, latter):
    return lax.psum_scatter(
        across(former, latter).astype(jnp.bfloat16), "out", scatter_dimension=0, tiled=True
    ).astype(jnp.float32)


def per_device(tokens, w_up, w_down, grad_out):
    features, grad_features = (
        lax.all_gather(tokens, "inp", axis=1, tiled=True),
        lax.all_gather(grad_out, "inp", axis=1, tiled=True),
    )
    up_block, down_block = (
        lax.all_gather(w_up, "out", axis=0, tiled=True),
        lax.all_gather(w_down, "out", axis=0, tiled=True),
    )
    hidden_partial = product(features, up_block)
    hidden = share_hidden(hidden_partial)
    activation = whole_hidden(gelu_value(hidden).astype(jnp.bfloat16))
    output = share_features(product(activation, down_block)).astype(jnp.bfloat16)
    up_again, down_again = (
        lax.all_gather(w_up, "out", axis=0, tiled=True),
        lax.all_gather(w_down, "out", axis=0, tiled=True),
    )
    act_partial = against(grad_features, down_again)
    grad_act = share_hidden(act_partial)
    grad_hidden = whole_hidden((grad_act * gelu_slope(hidden)).astype(jnp.bfloat16))
    grad_tokens = share_features(against(grad_hidden, up_again)).astype(jnp.bfloat16)
    grad_down = weight_grad(activation, grad_features).astype(jnp.bfloat16)
    grad_up = weight_grad(features, grad_hidden).astype(jnp.bfloat16)
    return (output, grad_tokens, grad_up, grad_down)


def solution(mesh):
    placed = (
        P("out", ("wgt", "inp")),
        P(("wgt", "out"), "inp"),
        P(("inp", "out"), "wgt"),
        P("out", ("wgt", "inp")),
    )
    return jax.shard_map(
        per_device,
        mesh=mesh,
        in_specs=placed,
        out_specs=(
            P("out", ("wgt", "inp")),
            P("out", ("wgt", "inp")),
            P(("wgt", "out"), "inp"),
            P(("inp", "out"), "wgt"),
        ),
        check_vma=False,
    )
```

profile of v0, /device:TPU:1, one launch (start us, length us, event | category | flops | bytes accessed | tf_op | source)
XLA Modules:
  0.0 491.5 jit_solution(3880922465054088078)
XLA Ops:
  7.2 0.0 copy-start.2
  7.2 0.0 all-gather.9.cloned.1.call-start
  7.2 0.7 all-gather.9.cloned.1.call-update
  7.9 0.0 all-gather.5.cloned.1.call-start
  8.0 0.7 all-gather.5.cloned.1.call-update
  8.7 0.0 reduce-scatter.21.cloned.1.call-start
  8.7 0.0 copy-done.2
  8.7 23.7 %all_gather.24 = bf16[256,768]{0,1:T(8,128)(2,1)S(1)} all-gather(bf16[256,96]{0,1:T(8,128)(2,1)S(1)} %copy-done.2), channel_id=1, replica_groups=mesh['inp'=8,'wgt'=8,'out'=4] {'inp'}, dimensions={1}, use_global_device_ids=true | all-gather | bytes 442368 | tf_op jit(solution)/shard_map/all_gather | solution.py:63
  32.4 25.7 %all-gather.9.cloned.1.call-done = bf16[3072,768]{1,0:T(8,128)(2,1)} async-done(((bf16[768,768]{1,0:T(8,128)(2,1)}), bf16[3072,768]{1,0:T(8,128)(2,1)}) %all-gather.9.cloned.1.call-update) | async-done | bytes 4718608 | tf_op jit(solution)/shard_map/all_gather | solution.py:67
  58.1 3.8 convolution_convert_fusion.2
  61.9 1.6 copy.12
  63.5 0.0 reduce-scatter.21.cloned.1.call-update
  63.5 0.0 reduce-scatter.19.cloned.1.call-start
  63.5 0.7 copy-done.3
  64.3 21.4 %all_gather.20 = bf16[256,768]{0,1:T(8,128)(2,1)S(1)} all-gather(bf16[256,96]{0,1:T(8,128)(2,1)S(1)} %copy-done.3), channel_id=1, replica_groups=mesh['inp'=8,'wgt'=8,'out'=4] {'inp'}, dimensions={1}, use_global_device_ids=true | all-gather | bytes 442368 | tf_op jit(solution)/shard_map/all_gather | solution.py:62
  85.6 17.8 %all-gather.5.cloned.1.call-done = bf16[768,3072]{1,0:T(8,128)(2,1)} async-done(((bf16[192,3072]{1,0:T(8,128)(2,1)}), bf16[768,3072]{1,0:T(8,128)(2,1)}) %all-gather.5.cloned.1.call-update) | async-done | bytes 4718608 | tf_op jit(solution)/shard_map/all_gather | solution.py:66
  103.5 3.7 convolution_convert_fusion.3
  107.2 1.6 copy.10
  108.8 0.0 reduce-scatter.19.cloned.1.call-update
  108.8 0.0 all-gather.11.cloned.1.call-start
  108.9 34.6 %reduce-scatter.21.cloned.1.call-done = bf16[384,256]{1,0:T(8,128)(2,1)} async-done(((bf16[3072,256]{1,0:T(8,128)(2,1)}), bf16[384,256]{1,0:T(8,128)(2,1)}) %reduce-scatter.21.cloned.1.call-update) | async-done | bytes 196624
  143.5 1.1 copy.13
  144.6 43.6 %reduce-scatter.19.cloned.1.call-done = bf16[384,256]{1,0:T(8,128)(2,1)} async-done(((bf16[3072,256]{1,0:T(8,128)(2,1)}), bf16[384,256]{1,0:T(8,128)(2,1)}) %reduce-scatter.19.cloned.1.call-update) | async-done | bytes 196624
  188.2 1.1 copy.11
  189.3 1.0 fusion.8
  190.3 0.0 all-gather.11.cloned.1.call-update
  190.4 0.0 all-gather.7.cloned.1.call-start
  190.4 0.5 all-gather.7.cloned.1.call-update
  190.9 0.0 reduce-scatter.15.cloned.1.call-start
  191.0 40.2 %all-gather.11.cloned.1.call-done = bf16[256,3072]{1,0:T(8,128)(2,1)} async-done(((bf16[256,384]{1,0:T(8,128)(2,1)}), bf16[256,3072]{1,0:T(8,128)(2,1)}) %all-gather.11.cloned.1.call-update) | async-done | bytes 1572880 | tf_op jit(solution)/shard_map/all_gather | solution.py:51
  231.2 5.0 %convolution_convert_fusion.4 = bf16[256,768]{0,1:T(8,128)(2,1)} fusion(bf16[256,3072]{1,0:T(8,128)(2,1)} %all-gather.11.cloned.1.call-done, bf16[768,3072]{1,0:T(8,128)(2,1)} %all-gather.5.cloned.1.call-done), kind=kOutput, calls=%fused_computation.5 | convolution fusion | flops 1208156160 | bytes 6684672 | tf_op jit(solution)/shard_map/dot_general | solution.py:27
  236.1 0.0 reduce-scatter.15.cloned.1.call-update
  236.2 0.0 reduce-scatter.13.cloned.1.call-start
  236.2 39.3 %all-gather.7.cloned.1.call-done = bf16[256,3072]{1,0:T(8,128)(2,1)} async-done(((bf16[256,384]{1,0:T(8,128)(2,1)}), bf16[256,3072]{1,0:T(8,128)(2,1)}) %all-gather.7.cloned.1.call-update) | async-done | bytes 1572880 | tf_op jit(solution)/shard_map/all_gather | solution.py:51
  275.5 5.6 %convolution_convert_fusion.5 = bf16[256,768]{0,1:T(8,128)(2,1)} fusion(bf16[256,3072]{1,0:T(8,128)(2,1)} %all-gather.7.cloned.1.call-done, bf16[3072,768]{1,0:T(8,128)(2,1)} %all-gather.9.cloned.1.call-done), kind=kOutput, calls=%fused_computation.6 | convolution fusion | flops 1208156160 | bytes 6684672 | tf_op jit(solution)/shard_map/dot_general | solution.py:23
  281.2 0.0 reduce-scatter.13.cloned.1.call-update
  281.2 0.0 reduce-scatter.17.cloned.1.call-start
  281.3 3.6 convolution_convert_fusion
  284.8 0.0 reduce-scatter.17.cloned.1.call-update
  284.9 0.0 reduce-scatter.23.cloned.1.call-start
  284.9 1.3 copy-done
  286.2 3.7 fusion
  289.9 6.7 %copy.14 = bf16[768,3072]{1,0:T(8,128)(2,1)} copy(bf16[768,3072]{0,1:T(8,128)(2,1)} %fusion) | data formatting | bytes 9437184
  296.6 0.0 reduce-scatter.23.cloned.1.call-update
  296.7 19.6 %reduce-scatter.15.cloned.1.call-done = bf16[256,96]{0,1:T(8,128)(2,1)} async-done(((bf16[256,768]{0,1:T(8,128)(2,1)}), bf16[256,96]{0,1:T(8,128)(2,1)}) %reduce-scatter.15.cloned.1.call-update) | async-done | bytes 49168 | tf_op jit(solution)/shard_map/reduce_scatter | solution.py:39
  316.3 38.9 %reduce-scatter.13.cloned.1.call-done = bf16[256,96]{0,1:T(8,128)(2,1)} async-done(((bf16[256,768]{0,1:T(8,128)(2,1)}), bf16[256,96]{0,1:T(8,128)(2,1)}) %reduce-scatter.13.cloned.1.call-update) | async-done | bytes 49168 | tf_op jit(solution)/shard_map/reduce_scatter | solution.py:39
  355.2 66.7 %reduce-scatter.17.cloned.1.call-done = bf16[768,768]{1,0:T(8,128)(2,1)} async-done(((bf16[3072,768]{1,0:T(8,128)(2,1)}), bf16[768,768]{1,0:T(8,128)(2,1)}) %reduce-scatter.17.cloned.1.call-update) | async-done | bytes 1179664 | tf_op jit(solution)/shard_map/reduce_scatter | solution.py:55
  421.9 62.8 %reduce-scatter.23.cloned.1.call-done = bf16[192,3072]{1,0:T(8,128)(2,1)} async-done(((bf16[768,3072]{1,0:T(8,128)(2,1)}), bf16[192,3072]{1,0:T(8,128)(2,1)}) %reduce-scatter.23.cloned.1.call-update) | async-done | bytes 1179664
  (4 shorter events, 0.0 us)
Async XLA Ops:
  7.2 1.5 copy-start.2
  7.2 50.9 %all-gather.9.cloned.1.call-start = ((), (), s32[]{:S(2)}) async-start(), calls=%async_computation.8 | async-start | bytes 5898240 | tf_op jit(solution)/shard_map/all_gather | solution.py:67
  7.9 95.6 %all-gather.5.cloned.1.call-start = ((), (), s32[]{:S(2)}) async-start(), calls=%async_computation.6 | async-start | bytes 5898240 | tf_op jit(solution)/shard_map/all_gather | solution.py:66
  8.7 134.8 %reduce-scatter.21.cloned.1.call-start = ((), (), s32[]{:S(2)}) async-start(), calls=%async_computation.14 | async-start | bytes 1769472
  63.5 0.8 copy-start.3
  63.5 124.7 %reduce-scatter.19.cloned.1.call-start = ((), (), s32[]{:S(2)}) async-start(), calls=%async_computation.13 | async-start | bytes 1769472
  108.8 122.4 %all-gather.11.cloned.1.call-start = ((), (), s32[]{:S(2)}) async-start(), calls=%async_computation.10 | async-start | bytes 1769472 | tf_op jit(solution)/shard_map/all_gather | solution.py:51
  190.4 85.2 %all-gather.7.cloned.1.call-start = ((), (), s32[]{:S(2)}) async-start(), calls=%async_computation.7 | async-start | bytes 1769472 | tf_op jit(solution)/shard_map/all_gather | solution.py:51
  190.9 125.4 %reduce-scatter.15.cloned.1.call-start = ((), (), s32[]{:S(2)}) async-start(), calls=%async_computation.11 | async-start | bytes 442368 | tf_op jit(solution)/shard_map/reduce_scatter | solution.py:39
  236.2 119.1 %reduce-scatter.13.cloned.1.call-start = ((), (), s32[]{:S(2)}) async-start(), calls=%async_computation.9 | async-start | bytes 442368 | tf_op jit(solution)/shard_map/reduce_scatter | solution.py:39
  275.5 5.7 %copy-start.1 = (bf16[256,3072]{1,0:T(8,128)(2,1)S(1)}, bf16[256,3072]{1,0:T(8,128)(2,1)}, u32[]{:S(2)}) copy-start(bf16[256,3072]{1,0:T(8,128)(2,1)} %all-gather.7.cloned.1.call-done) | copy-start | bytes 4718596
  281.2 140.7 %reduce-scatter.17.cloned.1.call-start = ((), (), s32[]{:S(2)}) async-start(), calls=%async_computation.12 | async-start | bytes 5898240 | tf_op jit(solution)/shard_map/reduce_scatter | solution.py:55
  284.8 1.4 copy-start
  284.9 199.8 %reduce-scatter.23.cloned.1.call-start = ((), (), s32[]{:S(2)}) async-start(), calls=%async_computation.15 | async-start | bytes 5898240
Sparse Core Ops, SparseCore 0:
  9.8 48.2 all-gather.8
  59.9 43.5 all-gather.4
  106.0 37.3 reduce-scatter.20
  145.9 42.2 reduce-scatter.18
  190.5 40.6 all-gather.10
  233.4 42.0 all-gather.6
  278.6 37.6 reduce-scatter.14
  319.5 35.6 reduce-scatter.12
  358.6 63.2 reduce-scatter.16
  425.3 59.3 reduce-scatter.22
where the time goes:
time: 492 us
  waiting for transfers between devices  391 us (79%)
  blocking collectives  45.1 us (9%)
  matrix products  25.4 us (5%)
  between operations  14.2 us (3%)
  local copies, waits for them, and re-layouts  14.1 us (3%)
    unnamed x13, waiting for transfers between devices  143 us
    all_gather x2, waiting for transfers between devices, whole_hidden(): return lax.all_gather(portion, 'wgt', axis=1, tiled=True)  79.5 us
    reduce_scatter x1, waiting for transfers between devices, weight_grad(): lax.psum_scatter(across(former, latter).astype(jnp.bfloat16), 'out', scat...  66.7 us
    reduce_scatter x2, waiting for transfers between devices, share_features(): lax.psum_scatter(partial_value.astype(jnp.bfloat16), 'inp', scatter_dimen...  58.6 us
    all_gather x1, waiting for transfers between devices, per_device(): lax.all_gather(w_down, 'out', axis=0, tiled=True)  25.7 us
    all_gather x1, blocking collectives, per_device(): lax.all_gather(grad_out, 'inp', axis=1, tiled=True)  23.7 us
    all_gather x1, blocking collectives, per_device(): lax.all_gather(tokens, 'inp', axis=1, tiled=True)  21.4 us
    all_gather x1, waiting for transfers between devices, per_device(): lax.all_gather(w_up, 'out', axis=0, tiled=True)  17.8 us
  transfers between devices with their start and end apart: 10, of which 10 were waited for; matrix products, arithmetic and copies ran while one was open for 7% of the time, Pallas kernels for 0%

commit v1 on v0

v1 whole, which is shorter than its diff:
```python
import jax
import jax.numpy as jnp
import numpy as np
from jax import lax
from jax.sharding import Mesh, PartitionSpec as P

tanh_scale = 0.7978845608028654
cubic_weight = 0.044715
pair = [(0, 1), (1, 0)]


def gelu_both(hidden):
    tangent = jnp.tanh(tanh_scale * (hidden + cubic_weight * hidden * hidden * hidden))
    value = 0.5 * hidden * (1.0 + tangent)
    slope = 0.5 * (1.0 + tangent) + 0.5 * hidden * (1.0 - tangent * tangent) * tanh_scale * (
        1.0 + 3.0 * cubic_weight * hidden * hidden
    )
    return value, slope


def contract(former, latter, former_dim, latter_dim):
    return lax.dot_general(
        former,
        latter,
        (((former_dim,), (latter_dim,)), ((), ())),
        preferred_element_type=jnp.float32,
    ).astype(jnp.bfloat16)


def swap(value, axis):
    return lax.ppermute(value, axis, pair)


def exchange(value, axis):
    return lax.all_to_all(value, axis, 0, 0, tiled=True)


def spread(value, axis, count):
    copies = jnp.broadcast_to(value[None], (count,) + value.shape)
    return exchange(copies, axis)


def share(value, axis, count):
    blocks = exchange(value.reshape((count, value.shape[0] // count) + value.shape[1:]), axis)
    return jnp.sum(blocks.astype(jnp.float32), axis=0)


def gathered(own):
    beside = swap(own, "core")
    across = swap(own, "xhi")
    beyond = swap(across, "core")
    return jnp.concatenate([beside, beyond, own, across], axis=0)


def scattered(former, latter, latter_dim):
    half = former.shape[0] // 2
    quarter = half // 2
    outgoing = contract(former[:half], latter, 1, latter_dim)
    kept = contract(former[half:], latter, 1, latter_dim)
    arrived = swap(outgoing, "core")
    total = kept.astype(jnp.float32) + arrived.astype(jnp.float32)
    crossing = swap(total[quarter:].astype(jnp.bfloat16), "xhi")
    return (total[:quarter] + crossing.astype(jnp.float32)).astype(jnp.bfloat16)


def orders(here):
    forth = [here ^ 1, here ^ 3, here, here ^ 2]
    back = [2 * (1 - ((here ^ j) & 1)) + ((here ^ j) >> 1) for j in range(4)]
    return forth, back


def reordered(array, blocks):
    size = array.shape[0] // 4
    return jnp.concatenate(
        [lax.dynamic_slice_in_dim(array, block * size, size, 0) for block in blocks], axis=0
    )


def per_device(tokens, w_up, w_down, grad_out):
    xhi, core = lax.axis_index("xhi"), lax.axis_index("core")
    blocks, places = orders(2 * xhi + core)
    up = gathered(w_up)
    down = gathered(w_down)
    both = jnp.concatenate([tokens.T, grad_out.T], axis=0)
    features = spread(both, "inp", 8).reshape(8, 2, 96, 256)
    x = reordered(features[:, 0].reshape(768, 256), blocks)
    g = features[:, 1].reshape(768, 256)

    hidden = share(contract(up, x, 0, 0), ("xlo", "y"), 8)
    value, slope = gelu_both(hidden)
    act = spread(value.astype(jnp.bfloat16), ("xlo", "y"), 8).reshape(3072, 256)

    grad_act_partial = contract(down, g, 1, 0)
    grad_act_rows = reordered(grad_act_partial, places)
    grad_act = share(grad_act_rows, ("xlo", "y"), 8)
    gh = spread((grad_act * slope).astype(jnp.bfloat16), ("xlo", "y"), 8).reshape(3072, 256)

    act_r = reordered(act, blocks)
    out = share(contract(down, act_r, 0, 0), "inp", 8).astype(jnp.bfloat16)
    grad_tok_partial = reordered(contract(up, gh, 1, 0), places)
    grad_tok = share(grad_tok_partial, "inp", 8).astype(jnp.bfloat16)
    grad_down = scattered(act_r, g, 1)
    grad_up = scattered(x, gh, 1)
    return (out.T, grad_tok.T, grad_up, grad_down)


def solution(mesh):
    fine = Mesh(
        np.asarray(mesh.devices).reshape(8, 2, 4, 2, 2), ("inp", "xlo", "y", "xhi", "core")
    )
    wgt, out = ("xlo", "y"), ("xhi", "core")
    tok = P(out, wgt + ("inp",))
    up = P(wgt + out, "inp")
    down = P(("inp",) + out, wgt)
    return jax.shard_map(
        per_device,
        mesh=fine,
        in_specs=(tok, up, down, tok),
        out_specs=(tok, tok, up, down),
        check_vma=False,
    )
```

time: 492 us -> 252 us (0.51)
  waiting for transfers between devices: 391 us -> 109 us
  starting transfers between devices: 0.4 us -> 53.9 us
  blocking collectives: 45.1 us -> 23.5 us
  between operations: 14.2 us -> 0.85 us
  other arithmetic: 1.05 us -> 13 us
  local copies, waits for them, and re-layouts: 14.1 us -> 23.7 us
    unnamed x13 -> x0, waiting for transfers between devices: 143 us -> none
    reduce_scatter x3 -> x0, waiting for transfers between devices: 125 us -> none  [the longest x1 66.7 us: weight_grad(): lax.psum_scatter(across(former, latter).astype(jnp.bfloat16), 'out', scat...]
    all_gather x4 -> x0, waiting for transfers between devices: 123 us -> none  [the longest x2 79.5 us: whole_hidden(): return lax.all_gather(portion, 'wgt', axis=1, tiled=True)]
    ppermute x0 -> x10, waiting for transfers between devices: none -> 56 us  [swap(): return lax.ppermute(value, axis, pair)]
    all_to_all x0 -> x6, waiting for transfers between devices: none -> 52.6 us  [exchange(): return lax.all_to_all(value, axis, 0, 0, tiled=True)]
    all_gather x2 -> x0, blocking collectives: 45.1 us -> none  [the longest x1 23.7 us: per_device(): lax.all_gather(grad_out, 'inp', axis=1, tiled=True)]
    all_to_all x0 -> x6, starting transfers between devices: none -> 30.8 us  [exchange(): return lax.all_to_all(value, axis, 0, 0, tiled=True)]
    all_to_all x0 -> x1, blocking collectives: none -> 23.5 us  [exchange(): return lax.all_to_all(value, axis, 0, 0, tiled=True)]
  transfers between devices with their start and end apart: 10 -> 16, of which waited for: 10 -> 9; matrix products, arithmetic and copies ran while one was open for 7% -> 21% of each run, Pallas kernels for 0% -> 0%
where the time goes in v1:
time: 252 us; the launch traced here: 251 us
  waiting for transfers between devices  109 us (43%)
  starting transfers between devices  53.9 us (21%)
  matrix products  27.3 us (11%)
  local copies, waits for them, and re-layouts  23.7 us (9%)
  blocking collectives  23.5 us (9%)
  other arithmetic  13 us (5%)
    ppermute x10, waiting for transfers between devices, swap(): return lax.ppermute(value, axis, pair)  56 us
    all_to_all x6, waiting for transfers between devices, exchange(): return lax.all_to_all(value, axis, 0, 0, tiled=True)  52.6 us
    all_to_all x6, starting transfers between devices, exchange(): return lax.all_to_all(value, axis, 0, 0, tiled=True)  30.8 us
    dot_general x8, matrix products, contract(): lax.dot_general(former, latter, (((former_dim,), (latter_dim,)), ((), ())...  27.3 us
    all_to_all x1, blocking collectives, exchange(): return lax.all_to_all(value, axis, 0, 0, tiled=True)  23.5 us
    ppermute x10, starting transfers between devices, swap(): return lax.ppermute(value, axis, pair)  23.2 us
    unnamed x40, local copies, waits for them, and re-layouts  15.7 us
    convert_element_type x2, other arithmetic, scattered(): return (total[:quarter] + crossing.astype(jnp.float32)).astype(jnp.bfloat16)  6.35 us
  transfers between devices with their start and end apart: 16, of which 9 were waited for; matrix products, arithmetic and copies ran while one was open for 21% of the time, Pallas kernels for 0%

profile of v1, /device:TPU:1, one launch (start us, length us, event | category | flops | bytes accessed | tf_op | source)
XLA Modules:
  0.0 251.0 jit_solution(12316236791428021030)
XLA Ops:
  0.6 3.7 %collective-permute-start.1 = (bf16[768,768]{1,0:T(8,128)(2,1)}, bf16[768,768]{1,0:T(8,128)(2,1)S(1)}, u32[]{:S(2)}, u32[]{:S(2)}) collective-permute-start(bf16[768,768]{1,0:T(8,128)(2,1)} %param.6), channel_id=1, source_target_pairs={{0,2},{2,0},{1,3},{3,1},{4,6},{6,4},{5,7},{7,5},{8,10},{10,8},{9,1... | collective-permute-start | bytes 3538952 | tf_op jit(solution)/shard_map/ppermute | solution.py:31
  4.4 3.1 %collective-permute-start = (bf16[768,768]{1,0:T(8,128)(2,1)}, bf16[768,768]{1,0:T(8,128)(2,1)}, u32[]{:S(2)}, u32[]{:S(2)}) collective-permute-start(bf16[768,768]{1,0:T(8,128)(2,1)} %param.6), channel_id=1, source_target_pairs={{0,1},{1,0},{2,3},{3,2},{4,5},{5,4},{6,7},{7,6},{8,9},{9,8},{10,11... | collective-permute-start | bytes 3538952 | tf_op jit(solution)/shard_map/ppermute | solution.py:31
  9.3 6.5 %all-to-all-start = ((bf16[8,192,256]{2,1,0:T(8,128)(2,1)}), bf16[8,192,256]{2,1,0:T(8,128)(2,1)S(1)}, u32[]{:S(2)}, u32[]{:S(2)}) async-start(bf16[8,192,256]{2,1,0:T(8,128)(2,1)} %broadcast_in_dim.6), calls=%async_computation | async-start | bytes 1572864 | tf_op jit(solution)/shard_map/all_to_all | solution.py:35
  15.7 13.5 %collective-permute-done.1 = bf16[768,768]{1,0:T(8,128)(2,1)S(1)} collective-permute-done((bf16[768,768]{1,0:T(8,128)(2,1)}, bf16[768,768]{1,0:T(8,128)(2,1)S(1)}, u32[]{:S(2)}, u32[]{:S(2)}) %collective-permute-start.1) | collective-permute-done | bytes 1179680 | tf_op jit(solution)/shard_map/ppermute | solution.py:31
  29.2 5.3 %collective-permute-start.2 = (bf16[768,768]{1,0:T(8,128)(2,1)S(1)}, bf16[768,768]{1,0:T(8,128)(2,1)S(1)}, u32[]{:S(2)}, u32[]{:S(2)}) collective-permute-start(bf16[768,768]{1,0:T(8,128)(2,1)S(1)} %collective-permute-done.1), channel_id=1, source_target_pairs={{0,1},{1,0},{2,3},{3,2},{4,5},{5,4},{6,7},{7,6},{8,9},{9,8},{10,11... | collective-permute-start | bytes 3538952 | tf_op jit(solution)/shard_map/ppermute | solution.py:31
  34.6 19.9 %collective-permute-done.4 = bf16[192,3072]{1,0:T(8,128)(2,1)} collective-permute-done((bf16[192,3072]{1,0:T(8,128)(2,1)}, bf16[192,3072]{1,0:T(8,128)(2,1)}, u32[]{:S(2)}, u32[]{:S(2)}) %collective-permute-start.4) | collective-permute-done | bytes 1179680 | tf_op jit(solution)/shard_map/ppermute | solution.py:31
  54.5 2.3 collective-permute-start.5
  56.8 2.4 constant_dynamic-update-slice_fusion.3
  59.2 2.4 constant_dynamic-update-slice_fusion.7
  62.4 1.1 constant_dynamic-update-slice_fusion.2
  63.5 1.2 constant_dynamic-update-slice_fusion.1
  64.7 1.2 constant_dynamic-update-slice_fusion
  65.9 3.7 %convolution_convert_fusion.2 = bf16[3072,256]{1,0:T(8,128)(2,1)S(1)} fusion(bf16[3072,768]{1,0:T(8,128)(2,1)} %constant_dynamic-update-slice_fusion, bf16[768,256]{1,0:T(8,128)(2,1)S(1)} %bitcast.27), kind=kOutput, calls=%fused_computation.4 | convolution fusion | flops 1208745984 | bytes 6684672 | tf_op jit(solution)/shard_map/dot_general | solution.py:22
  69.7 1.3 pad_maximum_fusion
  71.0 5.5 %all-to-all-start.4 = ((bf16[8,384,256]{2,1,0:T(8,128)(2,1)}), bf16[8,384,256]{2,1,0:T(8,128)(2,1)S(1)}, u32[]{:S(2)}, u32[]{:S(2)}) async-start(bf16[8,384,256]{2,1,0:T(8,128)(2,1)} %bitcast.9), calls=%async_computation.4 | async-start | bytes 3145728 | tf_op jit(solution)/shard_map/all_to_all | solution.py:35
  76.5 2.4 constant_dynamic-update-slice_fusion.6
  78.9 1.1 constant_dynamic-update-slice_fusion.5
  80.0 2.4 constant_dynamic-update-slice_fusion.4
  82.4 5.0 %convolution_convert_fusion.3 = bf16[3072,256]{1,0:T(8,128)(2,1)} fusion(bf16[768,3072]{1,0:T(8,128)(2,1)} %constant_dynamic-update-slice_fusion.4, bf16[192,256]{1,0:T(8,128)(2,1)S(1)} %copy-done.11, bf16[192,256]{1,0:T(8,128)(2,1)S(1)} %copy-done.13, bf16[192,256]{1,0:T(8,128)(2,1)S(1)} %copy-done.16, bf16[192,256]{1,0:T(8,128)(2,1)S(1)} %copy-done.15), kind=kOutput, calls=%fused_computation.5 | convolution fusion | flops 1210318848 | bytes 6684672 | tf_op jit(solution)/shard_map/dot_general | solution.py:22
  87.4 9.7 %all-to-all-done.4 = bf16[8,384,256]{2,1,0:T(8,128)(2,1)S(1)} async-done(((bf16[8,384,256]{2,1,0:T(8,128)(2,1)}), bf16[8,384,256]{2,1,0:T(8,128)(2,1)S(1)}, u32[]{:S(2)}, u32[]{:S(2)}) %all-to-all-start.4) | async-done | bytes 1572896 | tf_op jit(solution)/shard_map/all_to_all | solution.py:35
  97.1 3.6 %all-to-all-start.1 = ((bf16[8,384,256]{2,1,0:T(8,128)(2,1)}), bf16[8,384,256]{2,1,0:T(8,128)(2,1)S(1)}, u32[]{:S(2)}, u32[]{:S(2)}) async-start(bf16[8,384,256]{2,1,0:T(8,128)(2,1)} %bitcast.31), calls=%async_computation.1 | async-start | bytes 3145728 | tf_op jit(solution)/shard_map/all_to_all | solution.py:35
  100.7 1.0 convert_reduce_fusion
  101.7 19.6 %all-to-all-done.1 = bf16[8,384,256]{2,1,0:T(8,128)(2,1)S(1)} async-done(((bf16[8,384,256]{2,1,0:T(8,128)(2,1)}), bf16[8,384,256]{2,1,0:T(8,128)(2,1)S(1)}, u32[]{:S(2)}, u32[]{:S(2)}) %all-to-all-start.1) | async-done | bytes 1572896 | tf_op jit(solution)/shard_map/all_to_all | solution.py:35
  121.5 1.3 fusion.25
  122.9 23.5 %all_to_all.35 = bf16[8,384,256]{2,1,0:T(8,128)(2,1)S(1)} all-to-all(bf16[8,384,256]{2,1,0:T(8,128)(2,1)S(1)} %broadcast_in_dim.8), channel_id=1, replica_groups=mesh['inp'=8,'xlo'=2,'y'=4,'xhi'=2,'core'=2] {'xlo','y'}, dimensions={0} | all-to-all | bytes 3145728 | tf_op jit(solution)/shard_map/all_to_all | solution.py:35
  146.4 1.3 broadcast_in_dim.7
  147.7 3.6 %all-to-all-start.2 = ((bf16[8,384,256]{2,1,0:T(8,128)(2,1)}), bf16[8,384,256]{2,1,0:T(8,128)(2,1)S(1)}, u32[]{:S(2)}, u32[]{:S(2)}) async-start(bf16[8,384,256]{2,1,0:T(8,128)(2,1)} %broadcast_in_dim.7), calls=%async_computation.2 | async-start | bytes 3145728 | tf_op jit(solution)/shard_map/all_to_all | solution.py:35
  151.3 3.2 %convolution_convert_fusion = bf16[384,3072]{1,0:T(8,128)(2,1)} fusion(bf16[3072,256]{1,0:T(8,128)(2,1)S(1)} %bitcast.23, bf16[192,256]{1,0:T(8,128)(2,1)} %get-tuple-element.23, bf16[192,256]{1,0:T(8,128)(2,1)} %get-tuple-element.20), kind=kOutput, calls=%fused_computation.2 | convolution fusion | flops 605552640 | bytes 4128768 | tf_op jit(solution)/shard_map/dot_general | solution.py:22
  154.4 2.4 collective-permute-start.6
  156.8 14.5 %all-to-all-done.2 = bf16[8,384,256]{2,1,0:T(8,128)(2,1)S(1)} async-done(((bf16[8,384,256]{2,1,0:T(8,128)(2,1)}), bf16[8,384,256]{2,1,0:T(8,128)(2,1)S(1)}, u32[]{:S(2)}, u32[]{:S(2)}) %all-to-all-start.2) | async-done | bytes 1572896 | tf_op jit(solution)/shard_map/all_to_all | solution.py:35
  171.3 1.0 constant_dynamic-slice_fusion.11
  173.1 2.2 convolution_convert_fusion.4
  175.3 1.2 collective-permute-start.8
  176.5 3.7 %convolution_convert_fusion.6 = bf16[768,256]{1,0:T(8,128)(2,1)S(1)} fusion(bf16[768,3072]{1,0:T(8,128)(2,1)} %constant_dynamic-update-slice_fusion.4, bf16[3072,256]{1,0:T(8,128)(2,1)S(1)} %bitcast.24), kind=kOutput, calls=%fused_computation.26 | convolution fusion | flops 1208156160 | bytes 6684672 | tf_op jit(solution)/shard_map/dot_general | solution.py:22
  181.1 8.2 %all-to-all-start.6 = ((bf16[8,96,256]{2,1,0:T(8,128)(2,1)}), bf16[8,96,256]{2,1,0:T(8,128)(2,1)S(1)}, u32[]{:S(2)}, u32[]{:S(2)}) async-start(bf16[8,96,256]{2,1,0:T(8,128)(2,1)} %bitcast.11), calls=%async_computation.6 | async-start | bytes 786432 | tf_op jit(solution)/shard_map/all_to_all | solution.py:35
  189.3 2.5 convert_add_fusion.1
  191.8 2.1 copy-done
  194.1 2.5 %collective-permute-start.7 = (bf16[192,3072]{1,0:T(8,128)(2,1)S(1)}, bf16[192,3072]{1,0:T(8,128)(2,1)}, u32[]{:S(2)}, u32[]{:S(2)}) collective-permute-start(bf16[192,3072]{1,0:T(8,128)(2,1)S(1)} %slice.49), channel_id=1, source_target_pairs={{0,2},{2,0},{1,3},{3,1},{4,6},{6,4},{5,7},{7,5},{8,10},{10,8},{9,1... | collective-permute-start | bytes 3538952 | tf_op jit(solution)/shard_map/ppermute | solution.py:31
  196.6 4.5 %fusion.10 = bf16[768,256]{1,0:T(8,128)(2,1)} fusion(bf16[3072,768]{1,0:T(8,128)(2,1)} %constant_dynamic-update-slice_fusion, bf16[768,256]{1,0:T(8,128)(2,1)S(1)} %copy-done.3, bf16[768,256]{1,0:T(8,128)(2,1)S(1)} %copy-done.4, bf16[768,256]{1,0:T(8,128)(2,1)S(1)} %copy-done.8, bf16[768,256]{1,0:T(8,128)(2,1)S(1)} %copy-done.6), kind=kOutput, calls=%fused_computation.25 | convolution fusion | flops 1214447616 | bytes 6684672 | tf_op jit(solution)/shard_map/dot_general | solution.py:22
  201.2 3.3 %all-to-all-done.6 = bf16[8,96,256]{2,1,0:T(8,128)(2,1)S(1)} async-done(((bf16[8,96,256]{2,1,0:T(8,128)(2,1)}), bf16[8,96,256]{2,1,0:T(8,128)(2,1)S(1)}, u32[]{:S(2)}, u32[]{:S(2)}) %all-to-all-start.6) | async-done | bytes 393248 | tf_op jit(solution)/shard_map/all_to_all | solution.py:35
  204.4 3.5 %all-to-all-start.3 = ((bf16[8,96,256]{2,1,0:T(8,128)(2,1)}), bf16[8,96,256]{2,1,0:T(8,128)(2,1)S(1)}, u32[]{:S(2)}, u32[]{:S(2)}) async-start(bf16[8,96,256]{2,1,0:T(8,128)(2,1)} %bitcast.33), calls=%async_computation.3 | async-start | bytes 786432 | tf_op jit(solution)/shard_map/all_to_all | solution.py:35
  207.9 2.5 convert_add_fusion
  210.4 2.2 copy-done.1
  212.7 2.5 %collective-permute-start.9 = (bf16[768,768]{1,0:T(8,128)(2,1)S(1)}, bf16[768,768]{1,0:T(8,128)(2,1)}, u32[]{:S(2)}, u32[]{:S(2)}) collective-permute-start(bf16[768,768]{1,0:T(8,128)(2,1)S(1)} %slice.48), channel_id=1, source_target_pairs={{0,2},{2,0},{1,3},{3,1},{4,6},{6,4},{5,7},{7,5},{8,10},{10,8},{9,1... | collective-permute-start | bytes 3538952 | tf_op jit(solution)/shard_map/ppermute | solution.py:31
  215.9 5.5 %all-to-all-done.3 = bf16[8,96,256]{2,1,0:T(8,128)(2,1)S(1)} async-done(((bf16[8,96,256]{2,1,0:T(8,128)(2,1)}), bf16[8,96,256]{2,1,0:T(8,128)(2,1)S(1)}, u32[]{:S(2)}, u32[]{:S(2)}) %all-to-all-start.3) | async-done | bytes 393248 | tf_op jit(solution)/shard_map/all_to_all | solution.py:35
  223.1 3.7 %fusion.1 = bf16[192,3072]{1,0:T(8,128)(2,1)} fusion(f32[384,3072]{1,0:T(8,128)} %copy-done, bf16[192,3072]{1,0:T(8,128)(2,1)} %collective-permute-done.7), kind=kLoop, calls=%fused_computation.15 | loop fusion | flops 1769472 | bytes 4718592 | tf_op jit(solution)/shard_map/convert_element_type | solution.py:63
  226.8 21.6 %collective-permute-done.9 = bf16[768,768]{1,0:T(8,128)(2,1)} collective-permute-done((bf16[768,768]{1,0:T(8,128)(2,1)S(1)}, bf16[768,768]{1,0:T(8,128)(2,1)}, u32[]{:S(2)}, u32[]{:S(2)}) %collective-permute-start.9) | collective-permute-done | bytes 1179680 | tf_op jit(solution)/shard_map/ppermute | solution.py:31
  248.3 2.6 %fusion = bf16[768,768]{1,0:T(8,128)(2,1)} fusion(f32[1536,768]{1,0:T(8,128)S(1)} %copy-done.2, bf16[768,768]{1,0:T(8,128)(2,1)} %collective-permute-done.9), kind=kLoop, calls=%fused_computation.12 | loop fusion | flops 1769472 | bytes 4718592 | tf_op jit(solution)/shard_map/convert_element_type | solution.py:63
  (55 shorter events, 7.3 us)
Async XLA Ops:
  0.6 28.6 %collective-permute-start.1 = (bf16[768,768]{1,0:T(8,128)(2,1)}, bf16[768,768]{1,0:T(8,128)(2,1)S(1)}, u32[]{:S(2)}, u32[]{:S(2)}) collective-permute-start(bf16[768,768]{1,0:T(8,128)(2,1)} %param.6), channel_id=1, source_target_pairs={{0,2},{2,0},{1,3},{3,1},{4,6},{6,4},{5,7},{7,5},{8,10},{10,8},{9,1... | collective-permute-start | bytes 3538952 | tf_op jit(solution)/shard_map/ppermute | solution.py:31
  4.3 50.2 %collective-permute-start.4 = (bf16[192,3072]{1,0:T(8,128)(2,1)}, bf16[192,3072]{1,0:T(8,128)(2,1)}, u32[]{:S(2)}, u32[]{:S(2)}) collective-permute-start(bf16[192,3072]{1,0:T(8,128)(2,1)} %param.5), channel_id=1, source_target_pairs={{0,2},{2,0},{1,3},{3,1},{4,6},{6,4},{5,7},{7,5},{8,10},{10,8},{9,1... | collective-permute-start | bytes 3538952 | tf_op jit(solution)/shard_map/ppermute | solution.py:31
  4.4 52.4 %collective-permute-start = (bf16[768,768]{1,0:T(8,128)(2,1)}, bf16[768,768]{1,0:T(8,128)(2,1)}, u32[]{:S(2)}, u32[]{:S(2)}) collective-permute-start(bf16[768,768]{1,0:T(8,128)(2,1)} %param.6), channel_id=1, source_target_pairs={{0,1},{1,0},{2,3},{3,2},{4,5},{5,4},{6,7},{7,6},{8,9},{9,8},{10,11... | collective-permute-start | bytes 3538952 | tf_op jit(solution)/shard_map/ppermute | solution.py:31
  7.5 51.7 %collective-permute-start.3 = (bf16[192,3072]{1,0:T(8,128)(2,1)}, bf16[192,3072]{1,0:T(8,128)(2,1)}, u32[]{:S(2)}, u32[]{:S(2)}) collective-permute-start(bf16[192,3072]{1,0:T(8,128)(2,1)} %param.5), channel_id=1, source_target_pairs={{0,1},{1,0},{2,3},{3,2},{4,5},{5,4},{6,7},{7,6},{8,9},{9,8},{10,11... | collective-permute-start | bytes 3538952 | tf_op jit(solution)/shard_map/ppermute | solution.py:31
  9.3 52.3 %all-to-all-start = ((bf16[8,192,256]{2,1,0:T(8,128)(2,1)}), bf16[8,192,256]{2,1,0:T(8,128)(2,1)S(1)}, u32[]{:S(2)}, u32[]{:S(2)}) async-start(bf16[8,192,256]{2,1,0:T(8,128)(2,1)} %broadcast_in_dim.6), calls=%async_computation | async-start | bytes 1572864 | tf_op jit(solution)/shard_map/all_to_all | solution.py:35
  29.2 33.2 %collective-permute-start.2 = (bf16[768,768]{1,0:T(8,128)(2,1)S(1)}, bf16[768,768]{1,0:T(8,128)(2,1)S(1)}, u32[]{:S(2)}, u32[]{:S(2)}) collective-permute-start(bf16[768,768]{1,0:T(8,128)(2,1)S(1)} %collective-permute-done.1), channel_id=1, source_target_pairs={{0,1},{1,0},{2,3},{3,2},{4,5},{5,4},{6,7},{7,6},{8,9},{9,8},{10,11... | collective-permute-start | bytes 3538952 | tf_op jit(solution)/shard_map/ppermute | solution.py:31
  54.5 21.9 %collective-permute-start.5 = (bf16[192,3072]{1,0:T(8,128)(2,1)}, bf16[192,3072]{1,0:T(8,128)(2,1)}, u32[]{:S(2)}, u32[]{:S(2)}) collective-permute-start(bf16[192,3072]{1,0:T(8,128)(2,1)} %collective-permute-done.4), channel_id=1, source_target_pairs={{0,1},{1,0},{2,3},{3,2},{4,5},{5,4},{6,7},{7,6},{8,9},{9,8},{10,11... | collective-permute-start | bytes 3538952 | tf_op jit(solution)/shard_map/ppermute | solution.py:31
  61.6 1.9 copy-start.9
  71.0 7.9 %copy-start.10 = (bf16[192,3072]{1,0:T(8,128)(2,1)S(1)}, bf16[192,3072]{1,0:T(8,128)(2,1)}, u32[]{:S(2)}) copy-start(bf16[192,3072]{1,0:T(8,128)(2,1)} %param.5) | copy-start | bytes 3538948
  71.0 26.1 %all-to-all-start.4 = ((bf16[8,384,256]{2,1,0:T(8,128)(2,1)}), bf16[8,384,256]{2,1,0:T(8,128)(2,1)S(1)}, u32[]{:S(2)}, u32[]{:S(2)}) async-start(bf16[8,384,256]{2,1,0:T(8,128)(2,1)} %bitcast.9), calls=%async_computation.4 | async-start | bytes 3145728 | tf_op jit(solution)/shard_map/all_to_all | solution.py:35
  78.9 3.5 %copy-start.11 = (bf16[192,256]{1,0:T(8,128)(2,1)S(1)}, bf16[192,256]{1,0:T(8,128)(2,1)}, u32[]{:S(2)}) copy-start(bf16[192,256]{1,0:T(8,128)(2,1)} %get-tuple-element.21) | copy-start | bytes 294916
  78.9 3.5 %copy-start.13 = (bf16[192,256]{1,0:T(8,128)(2,1)S(1)}, bf16[192,256]{1,0:T(8,128)(2,1)}, u32[]{:S(2)}) copy-start(bf16[192,256]{1,0:T(8,128)(2,1)} %get-tuple-element.22) | copy-start | bytes 294916
  78.9 3.5 %copy-start.15 = (bf16[192,256]{1,0:T(8,128)(2,1)S(1)}, bf16[192,256]{1,0:T(8,128)(2,1)}, u32[]{:S(2)}) copy-start(bf16[192,256]{1,0:T(8,128)(2,1)} %get-tuple-element.20) | copy-start | bytes 294916
  78.9 3.5 %copy-start.16 = (bf16[192,256]{1,0:T(8,128)(2,1)S(1)}, bf16[192,256]{1,0:T(8,128)(2,1)}, u32[]{:S(2)}) copy-start(bf16[192,256]{1,0:T(8,128)(2,1)} %get-tuple-element.23) | copy-start | bytes 294916
  97.1 24.2 %all-to-all-start.1 = ((bf16[8,384,256]{2,1,0:T(8,128)(2,1)}), bf16[8,384,256]{2,1,0:T(8,128)(2,1)S(1)}, u32[]{:S(2)}, u32[]{:S(2)}) async-start(bf16[8,384,256]{2,1,0:T(8,128)(2,1)} %bitcast.31), calls=%async_computation.1 | async-start | bytes 3145728 | tf_op jit(solution)/shard_map/all_to_all | solution.py:35
  147.7 23.7 %all-to-all-start.2 = ((bf16[8,384,256]{2,1,0:T(8,128)(2,1)}), bf16[8,384,256]{2,1,0:T(8,128)(2,1)S(1)}, u32[]{:S(2)}, u32[]{:S(2)}) async-start(bf16[8,384,256]{2,1,0:T(8,128)(2,1)} %broadcast_in_dim.7), calls=%async_computation.2 | async-start | bytes 3145728 | tf_op jit(solution)/shard_map/all_to_all | solution.py:35
  154.4 34.8 %collective-permute-start.6 = (bf16[384,3072]{1,0:T(8,128)(2,1)}, bf16[384,3072]{1,0:T(8,128)(2,1)}, u32[]{:S(2)}, u32[]{:S(2)}) collective-permute-start(bf16[384,3072]{1,0:T(8,128)(2,1)} %convolution_convert_fusion), channel_id=1, source_target_pairs={{0,1},{1,0},{2,3},{3,2},{4,5},{5,4},{6,7},{7,6},{8,9},{9,8},{10,11... | collective-permute-start | bytes 7077896 | tf_op jit(solution)/shard_map/ppermute | solution.py:31
  172.3 0.8 copy-start.5
  172.3 3.0 %copy-start.7 = (bf16[768,256]{1,0:T(8,128)(2,1)}, bf16[768,256]{1,0:T(8,128)(2,1)S(1)}, u32[]{:S(2)}) copy-start(bf16[768,256]{1,0:T(8,128)(2,1)S(1)} %get-tuple-element.11) | copy-start | bytes 1179652
  175.3 32.6 %collective-permute-start.8 = (bf16[1536,768]{1,0:T(8,128)(2,1)}, bf16[1536,768]{1,0:T(8,128)(2,1)}, u32[]{:S(2)}, u32[]{:S(2)}) collective-permute-start(bf16[1536,768]{1,0:T(8,128)(2,1)} %convolution_convert_fusion.4), channel_id=1, source_target_pairs={{0,1},{1,0},{2,3},{3,2},{4,5},{5,4},{6,7},{7,6},{8,9},{9,8},{10,11... | collective-permute-start | bytes 7077896 | tf_op jit(solution)/shard_map/ppermute | solution.py:31
  180.2 9.0 %copy-start.12 = (bf16[192,256]{1,0:T(8,128)(2,1)S(1)}, bf16[192,256]{1,0:T(8,128)(2,1)}, u32[]{:S(2)}) copy-start(bf16[192,256]{1,0:T(8,128)(2,1)} %get-tuple-element.21) | copy-start | bytes 294916
  180.2 9.0 %copy-start.14 = (bf16[192,256]{1,0:T(8,128)(2,1)S(1)}, bf16[192,256]{1,0:T(8,128)(2,1)}, u32[]{:S(2)}) copy-start(bf16[192,256]{1,0:T(8,128)(2,1)} %get-tuple-element.22) | copy-start | bytes 294916
  181.1 23.4 %all-to-all-start.6 = ((bf16[8,96,256]{2,1,0:T(8,128)(2,1)}), bf16[8,96,256]{2,1,0:T(8,128)(2,1)S(1)}, u32[]{:S(2)}, u32[]{:S(2)}) async-start(bf16[8,96,256]{2,1,0:T(8,128)(2,1)} %bitcast.11), calls=%async_computation.6 | async-start | bytes 786432 | tf_op jit(solution)/shard_map/all_to_all | solution.py:35
  191.8 2.1 copy-start
  193.9 2.7 %copy-start.3 = (bf16[768,256]{1,0:T(8,128)(2,1)S(1)}, bf16[768,256]{1,0:T(8,128)(2,1)}, u32[]{:S(2)}) copy-start(bf16[768,256]{1,0:T(8,128)(2,1)} %get-tuple-element.9) | copy-start | bytes 1179652
  193.9 2.7 %copy-start.4 = (bf16[768,256]{1,0:T(8,128)(2,1)S(1)}, bf16[768,256]{1,0:T(8,128)(2,1)}, u32[]{:S(2)}) copy-start(bf16[768,256]{1,0:T(8,128)(2,1)} %get-tuple-element.10) | copy-start | bytes 1179652
  193.9 2.7 %copy-start.6 = (bf16[768,256]{1,0:T(8,128)(2,1)S(1)}, bf16[768,256]{1,0:T(8,128)(2,1)}, u32[]{:S(2)}) copy-start(bf16[768,256]{1,0:T(8,128)(2,1)} %copy-done.5) | copy-start | bytes 1179652
  193.9 2.7 %copy-start.8 = (bf16[768,256]{1,0:T(8,128)(2,1)S(1)}, bf16[768,256]{1,0:T(8,128)(2,1)}, u32[]{:S(2)}) copy-start(bf16[768,256]{1,0:T(8,128)(2,1)} %copy-done.7) | copy-start | bytes 1179652
  194.1 29.0 %collective-permute-start.7 = (bf16[192,3072]{1,0:T(8,128)(2,1)S(1)}, bf16[192,3072]{1,0:T(8,128)(2,1)}, u32[]{:S(2)}, u32[]{:S(2)}) collective-permute-start(bf16[192,3072]{1,0:T(8,128)(2,1)S(1)} %slice.49), channel_id=1, source_target_pairs={{0,2},{2,0},{1,3},{3,1},{4,6},{6,4},{5,7},{7,5},{8,10},{10,8},{9,1... | collective-permute-start | bytes 3538952 | tf_op jit(solution)/shard_map/ppermute | solution.py:31
  204.4 17.0 %all-to-all-start.3 = ((bf16[8,96,256]{2,1,0:T(8,128)(2,1)}), bf16[8,96,256]{2,1,0:T(8,128)(2,1)S(1)}, u32[]{:S(2)}, u32[]{:S(2)}) async-start(bf16[8,96,256]{2,1,0:T(8,128)(2,1)} %bitcast.33), calls=%async_computation.3 | async-start | bytes 786432 | tf_op jit(solution)/shard_map/all_to_all | solution.py:35
  210.4 2.2 copy-start.1
  212.7 35.6 %collective-permute-start.9 = (bf16[768,768]{1,0:T(8,128)(2,1)S(1)}, bf16[768,768]{1,0:T(8,128)(2,1)}, u32[]{:S(2)}, u32[]{:S(2)}) collective-permute-start(bf16[768,768]{1,0:T(8,128)(2,1)S(1)} %slice.48), channel_id=1, source_target_pairs={{0,2},{2,0},{1,3},{3,1},{4,6},{6,4},{5,7},{7,5},{8,10},{10,8},{9,1... | collective-permute-start | bytes 3538952 | tf_op jit(solution)/shard_map/ppermute | solution.py:31
  222.1 26.2 %copy-start.2 = (f32[1536,768]{1,0:T(8,128)S(1)}, f32[1536,768]{1,0:T(8,128)}, u32[]{:S(2)}) copy-start(f32[1536,768]{1,0:T(8,128)} %copy-done.1) | copy-start | bytes 14155780

commit v2 on v1

--- a/solution.py
+++ b/solution.py
@@ -76,32 +76,61 @@
     )
 
 
+def natural(own, other, place):
+    return jnp.where(place == 0, jnp.stack([own, other]), jnp.stack([other, own]))
+
+
+def pick(array, place):
+    return lax.dynamic_index_in_dim(array, place, 0, keepdims=False)
+
+
 def per_device(tokens, w_up, w_down, grad_out):
     xhi, core = lax.axis_index("xhi"), lax.axis_index("core")
     blocks, places = orders(2 * xhi + core)
-    up = gathered(w_up)
-    down = gathered(w_down)
+    wgt = ("xlo", "y")
     both = jnp.concatenate([tokens.T, grad_out.T], axis=0)
     features = spread(both, "inp", 8).reshape(8, 2, 96, 256)
+    up = gathered(w_up)
+    down = natural(w_down, swap(w_down, "core"), core).reshape(1536, 768)
     x = reordered(features[:, 0].reshape(768, 256), blocks)
-    g = features[:, 1].reshape(768, 256)
+    g_own = features[:, 1].reshape(768, 256)
+    g = natural(g_own, swap(g_own, "xhi"), xhi)
 
-    hidden = share(contract(up, x, 0, 0), ("xlo", "y"), 8)
+    hidden_partial = contract(up, x, 0, 0).reshape(2, 8, 192, 256).transpose(1, 0, 2, 3)
+    hidden = share(hidden_partial.reshape(3072, 256), wgt, 8).reshape(2, 192, 256)
     value, slope = gelu_both(hidden)
-    act = spread(value.astype(jnp.bfloat16), ("xlo", "y"), 8).reshape(3072, 256)
+    value = value.astype(jnp.bfloat16)
 
-    grad_act_partial = contract(down, g, 1, 0)
-    grad_act_rows = reordered(grad_act_partial, places)
-    grad_act = share(grad_act_rows, ("xlo", "y"), 8)
-    gh = spread((grad_act * slope).astype(jnp.bfloat16), ("xlo", "y"), 8).reshape(3072, 256)
+    act_partial = jnp.stack(
+        [contract(down, g[half], 1, 0).reshape(8, 192, 256) for half in range(2)]
+    )
+    payload = jnp.concatenate(
+        [act_partial, jnp.broadcast_to(value[:, None], (2, 8, 192, 256))], axis=2
+    )
+    arrived = exchange(payload.reshape(16, 384, 256), ("xhi",) + wgt).reshape(2, 8, 2, 192, 256)
+    grad_act = jnp.sum(arrived[:, :, 0].astype(jnp.float32), axis=1)
+    act = arrived[:, :, 1].reshape(2, 1536, 256)
 
-    act_r = reordered(act, blocks)
-    out = share(contract(down, act_r, 0, 0), "inp", 8).astype(jnp.bfloat16)
-    grad_tok_partial = reordered(contract(up, gh, 1, 0), places)
-    grad_tok = share(grad_tok_partial, "inp", 8).astype(jnp.bfloat16)
-    grad_down = scattered(act_r, g, 1)
+    gh = spread((grad_act * slope).astype(jnp.bfloat16), wgt, 8)
+    gh = gh.transpose(1, 0, 2, 3).reshape(3072, 256)
+
+    out_own = contract(down, pick(act, xhi), 0, 0)
+    out_other = swap(contract(down, pick(act, 1 - xhi), 0, 0), "xhi")
+    out = (out_own.astype(jnp.float32) + out_other.astype(jnp.float32)).astype(jnp.bfloat16)
+
+    act_wide = jnp.concatenate([act[0], act[1]], axis=1)
+    g_wide = jnp.concatenate([g[0], g[1]], axis=1)
+    act_far = lax.dynamic_slice_in_dim(act_wide, (1 - core) * 768, 768, 0)
+    act_near = lax.dynamic_slice_in_dim(act_wide, core * 768, 768, 0)
+    down_far = swap(contract(act_far, g_wide, 1, 1), "core")
+    down_near = contract(act_near, g_wide, 1, 1)
+    grad_down = (down_near.astype(jnp.float32) + down_far.astype(jnp.float32)).astype(jnp.bfloat16)
+
+    grad_tok = reordered(contract(up, gh, 1, 0), places)
+    last = jnp.concatenate([out.reshape(8, 96, 256), grad_tok.reshape(8, 96, 256)], axis=1)
+    last = share(last.reshape(1536, 256), "inp", 8).astype(jnp.bfloat16)
     grad_up = scattered(x, gh, 1)
-    return (out.T, grad_tok.T, grad_up, grad_down)
+    return (last[:96].T, last[96:].T, grad_up, grad_down)
 
 
 def solution(mesh):

time: 252 us -> 219 us (0.87)
  blocking collectives: 23.5 us -> 62.5 us
  waiting for transfers between devices: 109 us -> 74 us
  starting transfers between devices: 53.9 us -> 36.8 us
  matrix products: 27.3 us -> 18.4 us
  local copies, waits for them, and re-layouts: 23.7 us -> 15.9 us
  other arithmetic: 13 us -> 9.13 us
    all_to_all x1 -> x2, blocking collectives: 23.5 us -> 62.5 us  [exchange(): return lax.all_to_all(value, axis, 0, 0, tiled=True)]
    all_to_all x6 -> x3, waiting for transfers between devices: 52.6 us -> 18.8 us  [exchange(): return lax.all_to_all(value, axis, 0, 0, tiled=True)]
    all_to_all x6 -> x3, starting transfers between devices: 30.8 us -> 18.6 us  [exchange(): return lax.all_to_all(value, axis, 0, 0, tiled=True)]
    dot_general x8 -> x10, matrix products: 27.3 us -> 18.4 us  [contract(): lax.dot_general(former, latter, (((former_dim,), (latter_dim,)), ((), ())...]
    unnamed x40 -> x33, local copies, waits for them, and re-layouts: 15.7 us -> 8.48 us
    ppermute x10 -> x9, starting transfers between devices: 23.2 us -> 18.2 us  [swap(): return lax.ppermute(value, axis, pair)]
    convert_element_type x2 -> x1, other arithmetic: 6.35 us -> 2.95 us  [scattered(): return (total[:quarter] + crossing.astype(jnp.float32)).astype(jnp.bfloat16)]
    select_n x0 -> x2, other arithmetic: none -> 3.23 us  [natural(): jnp.where(place == 0, jnp.stack([own, other]), jnp.stack([other, own]))]
  transfers between devices with their start and end apart: 16 -> 12, of which waited for: 9 -> 6; matrix products, arithmetic and copies ran while one was open for 21% -> 15% of each run, Pallas kernels for 0% -> 0%
where the time goes in v2:
time: 219 us; the launch traced here: 218 us
  waiting for transfers between devices  74 us (34%)
  blocking collectives  62.5 us (29%)
  starting transfers between devices  36.8 us (17%)
  matrix products  18.4 us (8%)
  local copies, waits for them, and re-layouts  15.9 us (7%)
  other arithmetic  9.13 us (4%)
    all_to_all x2, blocking collectives, exchange(): return lax.all_to_all(value, axis, 0, 0, tiled=True)  62.5 us
    ppermute x9, waiting for transfers between devices, swap(): return lax.ppermute(value, axis, pair)  55.1 us
    all_to_all x3, waiting for transfers between devices, exchange(): return lax.all_to_all(value, axis, 0, 0, tiled=True)  18.8 us
    all_to_all x3, starting transfers between devices, exchange(): return lax.all_to_all(value, axis, 0, 0, tiled=True)  18.6 us
    dot_general x10, matrix products, contract(): lax.dot_general(former, latter, (((former_dim,), (latter_dim,)), ((), ())...  18.4 us
    ppermute x9, starting transfers between devices, swap(): return lax.ppermute(value, axis, pair)  18.2 us
    unnamed x33, local copies, waits for them, and re-layouts  8.48 us
  transfers between devices with their start and end apart: 12, of which 6 were waited for; matrix products, arithmetic and copies ran while one was open for 15% of the time, Pallas kernels for 0%

profile of v2, /device:TPU:1, one launch (start us, length us, event | category | flops | bytes accessed | tf_op | source)
XLA Modules:
  0.0 217.7 jit_solution(4500106212438355518)
XLA Ops:
  0.6 3.7 %collective-permute-start.3 = (bf16[192,3072]{1,0:T(8,128)(2,1)}, bf16[192,3072]{1,0:T(8,128)(2,1)}, u32[]{:S(2)}, u32[]{:S(2)}) collective-permute-start(bf16[192,3072]{1,0:T(8,128)(2,1)} %param.5), channel_id=1, source_target_pairs={{0,2},{2,0},{1,3},{3,1},{4,6},{6,4},{5,7},{7,5},{8,10},{10,8},{9,1... | collective-permute-start | bytes 3538952 | tf_op jit(solution)/shard_map/ppermute | solution.py:31
  4.3 1.0 collective-permute-start.2
  5.3 0.8 pad_maximum_fusion.6
  6.1 0.9 broadcast_in_dim.6
  7.0 8.2 %all-to-all-start = ((bf16[8,192,256]{2,1,0:T(8,128)(2,1)}), bf16[8,192,256]{2,1,0:T(8,128)(2,1)S(1)}, u32[]{:S(2)}, u32[]{:S(2)}) async-start(bf16[8,192,256]{2,1,0:T(8,128)(2,1)} %broadcast_in_dim.6), calls=%async_computation | async-start | bytes 1572864 | tf_op jit(solution)/shard_map/all_to_all | solution.py:35
  15.2 14.0 %collective-permute-done.3 = bf16[192,3072]{1,0:T(8,128)(2,1)} collective-permute-done((bf16[192,3072]{1,0:T(8,128)(2,1)}, bf16[192,3072]{1,0:T(8,128)(2,1)}, u32[]{:S(2)}, u32[]{:S(2)}) %collective-permute-start.3) | collective-permute-done | bytes 1179680 | tf_op jit(solution)/shard_map/ppermute | solution.py:31
  29.3 2.3 %collective-permute-start.4 = (bf16[192,3072]{1,0:T(8,128)(2,1)}, bf16[192,3072]{1,0:T(8,128)(2,1)}, u32[]{:S(2)}, u32[]{:S(2)}) collective-permute-start(bf16[192,3072]{1,0:T(8,128)(2,1)} %collective-permute-done.3), channel_id=1, source_target_pairs={{0,1},{1,0},{2,3},{3,2},{4,5},{5,4},{6,7},{7,6},{8,9},{9,8},{10,11... | collective-permute-start | bytes 3538952 | tf_op jit(solution)/shard_map/ppermute | solution.py:31
  31.6 1.1 constant_dynamic-update-slice_fusion.3
  32.7 6.2 %all-to-all-done = bf16[8,192,256]{2,1,0:T(8,128)(2,1)S(1)} async-done(((bf16[8,192,256]{2,1,0:T(8,128)(2,1)}), bf16[8,192,256]{2,1,0:T(8,128)(2,1)S(1)}, u32[]{:S(2)}, u32[]{:S(2)}) %all-to-all-start) | async-done | bytes 786464 | tf_op jit(solution)/shard_map/all_to_all | solution.py:35
  39.0 2.4 %constant_dynamic-update-slice_fusion.2 = bf16[768,3072]{1,0:T(8,128)(2,1)} fusion(bf16[768,3072]{1,0:T(8,128)(2,1)} %constant_dynamic-update-slice_fusion.3, bf16[192,3072]{1,0:T(8,128)(2,1)} %collective-permute-done.4), kind=kLoop, calls=%fused_computation.66 | loop fusion | bytes 2359296
  41.4 1.1 constant_dynamic-update-slice_fusion.1
  42.5 2.4 %constant_dynamic-update-slice_fusion = bf16[768,3072]{1,0:T(8,128)(2,1)} fusion(bf16[768,3072]{1,0:T(8,128)(2,1)} %constant_dynamic-update-slice_fusion.1, bf16[192,3072]{1,0:T(8,128)(2,1)} %collective-permute-done.3), kind=kLoop, calls=%fused_computation.64 | loop fusion | bytes 2359296 | tf_op jit(solution)/shard_map/concatenate | solution.py:52
  44.9 3.8 %convolution_convert_fusion.2 = bf16[3072,256]{1,0:T(8,128)(2,1)S(1)} fusion(bf16[768,3072]{1,0:T(8,128)(2,1)} %constant_dynamic-update-slice_fusion, bf16[192,256]{1,0:T(8,128)(2,1)S(1)} %get-tuple-element.15, bf16[192,256]{1,0:T(8,128)(2,1)S(1)} %get-tuple-element.16, bf16[192,256]{1,0:T(8,128)(2,1)S(1)} %get-tuple-element.17, ...), kind=kOutput, calls=%fused_computation.3 | convolution fusion | flops 1210318848 | bytes 6684672 | tf_op jit(solution)/shard_map/dot_general | solution.py:22
  48.7 1.3 copy.9
  49.9 4.2 %all-to-all-start.1 = ((bf16[8,384,256]{2,1,0:T(8,128)(2,1)}), bf16[8,384,256]{2,1,0:T(8,128)(2,1)S(1)}, u32[]{:S(2)}, u32[]{:S(2)}) async-start(bf16[8,384,256]{2,1,0:T(8,128)(2,1)} %bitcast.16), calls=%async_computation.1 | async-start | bytes 3145728 | tf_op jit(solution)/shard_map/all_to_all | solution.py:35
  54.1 1.7 collective-permute-start.1
  55.9 2.0 maximum_select_fusion
  57.9 24.0 %collective-permute-done.1 = bf16[768,256]{1,0:T(8,128)(2,1)} collective-permute-done((bf16[768,256]{1,0:T(8,128)(2,1)S(1)}, bf16[768,256]{1,0:T(8,128)(2,1)}, u32[]{:S(2)}, u32[]{:S(2)}) %collective-permute-start.1) | collective-permute-done | bytes 393248 | tf_op jit(solution)/shard_map/ppermute | solution.py:31
  81.9 1.2 maximum_select_fusion.1
  83.1 0.8 convolution_convert_fusion.3
  84.0 0.8 convolution_convert_fusion.4
  84.8 0.2 convert_reduce_fusion.1
  85.3 0.2 pad_maximum_fusion
  85.5 42.9 %all_to_all.25 = bf16[16,384,256]{2,1,0:T(8,128)(2,1)S(1)} all-to-all(bf16[16,384,256]{2,1,0:T(8,128)(2,1)S(1)} %bitcast.58), channel_id=1, replica_groups=mesh['inp'=8,'xlo'=2,'y'=4,'xhi'=2,'core'=2] {'xhi','xlo','y'}, dimensions={0} | all-to-all | bytes 6291456 | tf_op jit(solution)/shard_map/all_to_all | solution.py:35
  128.6 0.3 fusion.18
  129.0 19.6 %all_to_all.26 = bf16[8,2,192,256]{3,2,1,0:T(8,128)(2,1)S(1)} all-to-all(bf16[8,2,192,256]{3,2,1,0:T(8,128)(2,1)S(1)} %broadcast_in_dim.8), channel_id=1, replica_groups=mesh['inp'=8,'xlo'=2,'y'=4,'xhi'=2,'core'=2] {'xlo','y'}, dimensions={0} | all-to-all | bytes 3145728 | tf_op jit(solution)/shard_map/all_to_all | solution.py:35
  148.8 1.1 copy-done.1
  149.9 2.2 %convolution_convert_fusion = bf16[384,3072]{1,0:T(8,128)(2,1)} fusion(bf16[3072,256]{1,0:T(8,128)(2,1)S(1)} %bitcast.55, bf16[192,256]{1,0:T(8,128)(2,1)S(1)} %get-tuple-element.17, bf16[192,256]{1,0:T(8,128)(2,1)S(1)} %get-tuple-element.14), kind=kOutput, calls=%fused_computation.1 | convolution fusion | flops 605552640 | bytes 4128768 | tf_op jit(solution)/shard_map/dot_general | solution.py:22
  152.1 5.0 %collective-permute-start.6 = (bf16[384,3072]{1,0:T(8,128)(2,1)}, bf16[384,3072]{1,0:T(8,128)(2,1)}, u32[]{:S(2)}, u32[]{:S(2)}) collective-permute-start(bf16[384,3072]{1,0:T(8,128)(2,1)} %convolution_convert_fusion), channel_id=1, source_target_pairs={{0,1},{1,0},{2,3},{3,2},{4,5},{5,4},{6,7},{7,6},{8,9},{9,8},{10,11... | collective-permute-start | bytes 7077896 | tf_op jit(solution)/shard_map/ppermute | solution.py:31
  157.2 1.3 slice_bitcast_fusion.1
  158.7 0.4 copy-done.5
  159.1 0.8 convolution_convert_fusion.8
  159.9 1.6 collective-permute-start.5
  161.7 1.8 convolution_convert_fusion.5
  163.5 0.3 collective-permute-start.8
  163.8 8.6 %collective-permute-done.5 = bf16[768,256]{1,0:T(8,128)(2,1)S(1)} collective-permute-done((bf16[768,256]{1,0:T(8,128)(2,1)S(1)}, bf16[768,256]{1,0:T(8,128)(2,1)S(1)}, u32[]{:S(2)}, u32[]{:S(2)}) %collective-permute-start.5) | collective-permute-done | bytes 393248 | tf_op jit(solution)/shard_map/ppermute | solution.py:31
  172.4 0.8 fusion.3
  173.3 1.4 convolution_convert_fusion.7
  174.8 0.9 pad_maximum_fusion.1
  175.7 6.2 %all-to-all-start.4 = ((bf16[8,192,256]{2,1,0:T(8,128)(2,1)}), bf16[8,192,256]{2,1,0:T(8,128)(2,1)S(1)}, u32[]{:S(2)}, u32[]{:S(2)}) async-start(bf16[8,192,256]{2,1,0:T(8,128)(2,1)} %pad_maximum_fusion.1), calls=%async_computation.4 | async-start | bytes 1572864 | tf_op jit(solution)/shard_map/all_to_all | solution.py:35
  182.0 2.5 %convert_add_fusion = f32[384,3072]{1,0:T(8,128)S(1)} fusion(bf16[384,3072]{1,0:T(8,128)(2,1)} %collective-permute-done.6, bf16[3072,256]{1,0:T(8,128)(2,1)S(1)} %bitcast.57, bf16[192,256]{1,0:T(8,128)(2,1)S(1)} %get-tuple-element.15, bf16[192,256]{1,0:T(8,128)(2,1)S(1)} %get-tuple-element.16), kind=kOutput, calls=%fused_computation | convolution fusion | flops 609091584 | bytes 8847360 | tf_op jit(solution)/shard_map/dot_general | solution.py:22
  184.4 2.1 copy-done
  186.7 2.7 %collective-permute-start.7 = (bf16[192,3072]{1,0:T(8,128)(2,1)S(1)}, bf16[192,3072]{1,0:T(8,128)(2,1)S(1)}, u32[]{:S(2)}, u32[]{:S(2)}) collective-permute-start(bf16[192,3072]{1,0:T(8,128)(2,1)S(1)} %slice.82), channel_id=1, source_target_pairs={{0,2},{2,0},{1,3},{3,1},{4,6},{6,4},{5,7},{7,5},{8,10},{10,8},{9,1... | collective-permute-start | bytes 3538952 | tf_op jit(solution)/shard_map/ppermute | solution.py:31
  189.4 3.5 %add_convert_fusion = bf16[768,768]{1,0:T(8,128)(2,1)} fusion(bf16[768,768]{1,0:T(8,128)(2,1)} %collective-permute-done.8, s32[]{:T(128)S(6)} %select_n.90, bf16[1536,256]{1,0:T(8,128)(2,1)} %bitcast.79, bf16[1536,256]{1,0:T(8,128)(2,1)} %bitcast.77, bf16[768,256]{1,0:T(8,128)(2,1)} %copy-done.12, bf16[768,256]{1,0:T(8,128)(2,1)S(1)} %copy-done.11), kind=kOutput, calls=%fused_computation.13 | convolution fusion | flops 610074624 | bytes 4718596 | tf_op jit(solution)/shard_map/dot_general | solution.py:22
  192.9 12.6 %all-to-all-done.4 = bf16[8,192,256]{2,1,0:T(8,128)(2,1)S(1)} async-done(((bf16[8,192,256]{2,1,0:T(8,128)(2,1)}), bf16[8,192,256]{2,1,0:T(8,128)(2,1)S(1)}, u32[]{:S(2)}, u32[]{:S(2)}) %all-to-all-start.4) | async-done | bytes 786464 | tf_op jit(solution)/shard_map/all_to_all | solution.py:35
  205.6 0.6 slice_bitcast_fusion.2
  206.3 8.5 %collective-permute-done.7 = bf16[192,3072]{1,0:T(8,128)(2,1)S(1)} collective-permute-done((bf16[192,3072]{1,0:T(8,128)(2,1)S(1)}, bf16[192,3072]{1,0:T(8,128)(2,1)S(1)}, u32[]{:S(2)}, u32[]{:S(2)}) %collective-permute-start.7) | collective-permute-done | bytes 1179680 | tf_op jit(solution)/shard_map/ppermute | solution.py:31
  214.7 2.9 %fusion = bf16[192,3072]{1,0:T(8,128)(2,1)} fusion(f32[384,3072]{1,0:T(8,128)} %copy-done, bf16[192,3072]{1,0:T(8,128)(2,1)S(1)} %collective-permute-done.7), kind=kLoop, calls=%fused_computation.11 | loop fusion | flops 1769472 | bytes 4718592 | tf_op jit(solution)/shard_map/convert_element_type | solution.py:63
  (48 shorter events, 1.5 us)
Async XLA Ops:
  0.6 30.9 %copy-start.6 = (bf16[768,768]{1,0:T(8,128)(2,1)S(1)}, bf16[768,768]{1,0:T(8,128)(2,1)}, u32[]{:S(2)}) copy-start(bf16[768,768]{1,0:T(8,128)(2,1)} %param.6) | copy-start | bytes 3538948
  0.6 28.6 %collective-permute-start.3 = (bf16[192,3072]{1,0:T(8,128)(2,1)}, bf16[192,3072]{1,0:T(8,128)(2,1)}, u32[]{:S(2)}, u32[]{:S(2)}) collective-permute-start(bf16[192,3072]{1,0:T(8,128)(2,1)} %param.5), channel_id=1, source_target_pairs={{0,2},{2,0},{1,3},{3,1},{4,6},{6,4},{5,7},{7,5},{8,10},{10,8},{9,1... | collective-permute-start | bytes 3538952 | tf_op jit(solution)/shard_map/ppermute | solution.py:31
  4.3 27.3 %collective-permute-start.2 = (bf16[192,3072]{1,0:T(8,128)(2,1)}, bf16[192,3072]{1,0:T(8,128)(2,1)S(1)}, u32[]{:S(2)}, u32[]{:S(2)}) collective-permute-start(bf16[192,3072]{1,0:T(8,128)(2,1)} %param.5), channel_id=1, source_target_pairs={{0,1},{1,0},{2,3},{3,2},{4,5},{5,4},{6,7},{7,6},{8,9},{9,8},{10,11... | collective-permute-start | bytes 3538952 | tf_op jit(solution)/shard_map/ppermute | solution.py:31
  7.0 31.8 %all-to-all-start = ((bf16[8,192,256]{2,1,0:T(8,128)(2,1)}), bf16[8,192,256]{2,1,0:T(8,128)(2,1)S(1)}, u32[]{:S(2)}, u32[]{:S(2)}) async-start(bf16[8,192,256]{2,1,0:T(8,128)(2,1)} %broadcast_in_dim.6), calls=%async_computation | async-start | bytes 1572864 | tf_op jit(solution)/shard_map/all_to_all | solution.py:35
  29.3 9.7 %collective-permute-start.4 = (bf16[192,3072]{1,0:T(8,128)(2,1)}, bf16[192,3072]{1,0:T(8,128)(2,1)}, u32[]{:S(2)}, u32[]{:S(2)}) collective-permute-start(bf16[192,3072]{1,0:T(8,128)(2,1)} %collective-permute-done.3), channel_id=1, source_target_pairs={{0,1},{1,0},{2,3},{3,2},{4,5},{5,4},{6,7},{7,6},{8,9},{9,8},{10,11... | collective-permute-start | bytes 3538952 | tf_op jit(solution)/shard_map/ppermute | solution.py:31
  31.5 24.3 %collective-permute-start = (bf16[768,768]{1,0:T(8,128)(2,1)S(1)}, bf16[768,768]{1,0:T(8,128)(2,1)}, u32[]{:S(2)}, u32[]{:S(2)}) collective-permute-start(bf16[768,768]{1,0:T(8,128)(2,1)S(1)} %copy-done.6), channel_id=1, source_target_pairs={{0,1},{1,0},{2,3},{3,2},{4,5},{5,4},{6,7},{7,6},{8,9},{9,8},{10,11... | collective-permute-start | bytes 3538952 | tf_op jit(solution)/shard_map/ppermute | solution.py:31
  38.9 2.6 %copy-start.7 = (bf16[192,3072]{1,0:T(8,128)(2,1)S(1)}, bf16[192,3072]{1,0:T(8,128)(2,1)}, u32[]{:S(2)}) copy-start(bf16[192,3072]{1,0:T(8,128)(2,1)} %param.5) | copy-start | bytes 3538948
  49.9 34.8 %all-to-all-start.1 = ((bf16[8,384,256]{2,1,0:T(8,128)(2,1)}), bf16[8,384,256]{2,1,0:T(8,128)(2,1)S(1)}, u32[]{:S(2)}, u32[]{:S(2)}) async-start(bf16[8,384,256]{2,1,0:T(8,128)(2,1)} %bitcast.16), calls=%async_computation.1 | async-start | bytes 3145728 | tf_op jit(solution)/shard_map/all_to_all | solution.py:35
  54.1 27.7 %collective-permute-start.1 = (bf16[768,256]{1,0:T(8,128)(2,1)S(1)}, bf16[768,256]{1,0:T(8,128)(2,1)}, u32[]{:S(2)}, u32[]{:S(2)}) collective-permute-start(bf16[768,256]{1,0:T(8,128)(2,1)S(1)} %bitcast.71), channel_id=1, source_target_pairs={{0,2},{2,0},{1,3},{3,1},{4,6},{6,4},{5,7},{7,5},{8,10},{10,8},{9,1... | collective-permute-start | bytes 1179656 | tf_op jit(solution)/shard_map/ppermute | solution.py:31
  57.9 26.0 %copy-start.4 = (bf16[2,768,768]{2,1,0:T(8,128)(2,1)}, bf16[2,768,768]{2,1,0:T(8,128)(2,1)S(1)}, u32[]{:S(2)}) copy-start(bf16[2,768,768]{2,1,0:T(8,128)(2,1)S(1)} %maximum_select_fusion) | copy-start | bytes 7077892
  83.1 0.9 copy-start.3
  148.8 1.2 copy-start.1
  152.1 29.8 %collective-permute-start.6 = (bf16[384,3072]{1,0:T(8,128)(2,1)}, bf16[384,3072]{1,0:T(8,128)(2,1)}, u32[]{:S(2)}, u32[]{:S(2)}) collective-permute-start(bf16[384,3072]{1,0:T(8,128)(2,1)} %convolution_convert_fusion), channel_id=1, source_target_pairs={{0,1},{1,0},{2,3},{3,2},{4,5},{5,4},{6,7},{7,6},{8,9},{9,8},{10,11... | collective-permute-start | bytes 7077896 | tf_op jit(solution)/shard_map/ppermute | solution.py:31
  157.2 1.9 copy-start.5
  158.5 3.1 %copy-start.10 = (bf16[768,256]{1,0:T(8,128)(2,1)}, bf16[768,256]{1,0:T(8,128)(2,1)S(1)}, u32[]{:S(2)}) copy-start(bf16[768,256]{1,0:T(8,128)(2,1)S(1)} %get-tuple-element.6) | copy-start | bytes 1179652
  158.5 3.1 %copy-start.12 = (bf16[768,256]{1,0:T(8,128)(2,1)}, bf16[768,256]{1,0:T(8,128)(2,1)S(1)}, u32[]{:S(2)}) copy-start(bf16[768,256]{1,0:T(8,128)(2,1)S(1)} %get-tuple-element.7) | copy-start | bytes 1179652
  159.9 12.5 %collective-permute-start.5 = (bf16[768,256]{1,0:T(8,128)(2,1)S(1)}, bf16[768,256]{1,0:T(8,128)(2,1)S(1)}, u32[]{:S(2)}, u32[]{:S(2)}) collective-permute-start(bf16[768,256]{1,0:T(8,128)(2,1)S(1)} %convolution_convert_fusion.8), channel_id=1, source_target_pairs={{0,2},{2,0},{1,3},{3,1},{4,6},{6,4},{5,7},{7,5},{8,10},{10,8},{9,1... | collective-permute-start | bytes 1179656 | tf_op jit(solution)/shard_map/ppermute | solution.py:31
  161.5 11.8 %slice-start = ((s8[4718592]{0:T(1024)(128)(4,1)}), s8[4194304]{0:T(1024)(128)(4,1)S(1)}, s32[]{:S(2)}) async-start(s8[4718592]{0:T(1024)(128)(4,1)} %bitcast.81), calls=%async_computation.5 | async-start | bytes 8388608
  161.6 1.9 copy-start.8
  161.6 1.9 copy-start.9
  161.7 11.6 %slice-start.1 = ((s8[4718592]{0:T(1024)(128)(4,1)}), s8[524288]{0:T(1024)(128)(4,1)S(1)}, s32[]{:S(2)}) async-start(s8[4718592]{0:T(1024)(128)(4,1)} %bitcast.81), calls=%async_computation.6 | async-start | bytes 1048576
  163.5 9.8 %copy-start.2 = (bf16[8,2,192,256]{3,2,0,1:T(8,128)(2,1)S(1)}, bf16[8,2,192,256]{3,2,0,1:T(8,128)(2,1)}, u32[]{:S(2)}) copy-start(bf16[8,2,192,256]{3,2,0,1:T(8,128)(2,1)} %copy-done.1) | copy-start | bytes 4718596
  163.5 25.9 %collective-permute-start.8 = (bf16[768,768]{1,0:T(8,128)(2,1)}, bf16[768,768]{1,0:T(8,128)(2,1)}, u32[]{:S(2)}, u32[]{:S(2)}) collective-permute-start(bf16[768,768]{1,0:T(8,128)(2,1)} %convolution_convert_fusion.5), channel_id=1, source_target_pairs={{0,1},{1,0},{2,3},{3,2},{4,5},{5,4},{6,7},{7,6},{8,9},{9,8},{10,11... | collective-permute-start | bytes 3538952 | tf_op jit(solution)/shard_map/ppermute | solution.py:31
  175.7 29.8 %all-to-all-start.4 = ((bf16[8,192,256]{2,1,0:T(8,128)(2,1)}), bf16[8,192,256]{2,1,0:T(8,128)(2,1)S(1)}, u32[]{:S(2)}, u32[]{:S(2)}) async-start(bf16[8,192,256]{2,1,0:T(8,128)(2,1)} %pad_maximum_fusion.1), calls=%async_computation.4 | async-start | bytes 1572864 | tf_op jit(solution)/shard_map/all_to_all | solution.py:35
  184.4 2.1 copy-start
  186.6 2.8 %copy-start.11 = (bf16[768,256]{1,0:T(8,128)(2,1)S(1)}, bf16[768,256]{1,0:T(8,128)(2,1)}, u32[]{:S(2)}) copy-start(bf16[768,256]{1,0:T(8,128)(2,1)} %copy-done.10) | copy-start | bytes 1179652
  186.7 28.0 %collective-permute-start.7 = (bf16[192,3072]{1,0:T(8,128)(2,1)S(1)}, bf16[192,3072]{1,0:T(8,128)(2,1)S(1)}, u32[]{:S(2)}, u32[]{:S(2)}) collective-permute-start(bf16[192,3072]{1,0:T(8,128)(2,1)S(1)} %slice.82), channel_id=1, source_target_pairs={{0,2},{2,0},{1,3},{3,1},{4,6},{6,4},{5,7},{7,5},{8,10},{10,8},{9,1... | collective-permute-start | bytes 3538952 | tf_op jit(solution)/shard_map/ppermute | solution.py:31

commit v3 on v1

v3 whole, which is shorter than its diff:
```python
import jax
import jax.numpy as jnp
import numpy as np
from jax import lax
from jax.experimental import pallas as pl
from jax.experimental.pallas import tpu as pltpu
from jax.sharding import Mesh, PartitionSpec as P

tanh_scale = 0.7978845608028654
cubic_weight = 0.044715
pair = [(0, 1), (1, 0)]
wgt = ("xlo", "y")
bf16, f32 = jnp.bfloat16, jnp.float32


def gelu_both(hidden):
    tangent = jnp.tanh(tanh_scale * (hidden + cubic_weight * hidden * hidden * hidden))
    value = 0.5 * hidden * (1.0 + tangent)
    slope = 0.5 * (1.0 + tangent) + 0.5 * hidden * (1.0 - tangent * tangent) * tanh_scale * (
        1.0 + 3.0 * cubic_weight * hidden * hidden
    )
    return value, slope


def dot(former, latter, former_dim, latter_dim):
    return lax.dot_general(
        former,
        latter,
        (((former_dim,), (latter_dim,)), ((), ())),
        preferred_element_type=f32,
    )


def contract(former, latter, former_dim, latter_dim):
    return dot(former, latter, former_dim, latter_dim).astype(bf16)


def swap(value, axis):
    return lax.ppermute(value, axis, pair)


def exchange(value, axis):
    return lax.all_to_all(value, axis, 0, 0, tiled=True)


def natural(own, other, place):
    return jnp.where(place == 0, jnp.stack([own, other]), jnp.stack([other, own]))


def local(kernel, outs, flops, moved, *operands):
    whole = pl.BlockSpec(memory_space=pltpu.VMEM)
    return pl.pallas_call(
        kernel,
        out_shape=[jax.ShapeDtypeStruct(shape, kind) for shape, kind in outs],
        in_specs=[pl.BlockSpec(memory_space=pltpu.SMEM)] + [whole] * (len(operands) - 1),
        out_specs=[whole] * len(outs),
        compiler_params=pltpu.CompilerParams(vmem_limit_bytes=40 * 1024 * 1024),
        cost_estimate=pl.CostEstimate(flops=flops, bytes_accessed=moved, transcendentals=0),
    )(*operands)


def feature_rows(features, block):
    return features[pl.ds(2 * block, 2), 0:96, :].reshape(192, 256)


def hidden_kernel(where, features, w0, w1, w2, w3, out):
    turned = [feature_rows(features, where[b]).T for b in range(4)]
    for chunk in range(8):
        columns = slice(384 * chunk, 384 * chunk + 384)
        total = dot(turned[0], w0[:, columns], 1, 0)
        for b, weights in ((1, w1), (2, w2), (3, w3)):
            total += dot(turned[b], weights[:, columns], 1, 0)
        rows = total.T.astype(bf16)
        half, target = chunk // 4, 2 * (chunk % 4)
        span = slice(192 * half, 192 * half + 192)
        out[target, span, :] = rows[:192]
        out[target + 1, span, :] = rows[192:]


def gelu_kernel(where, arrived, first, second, payload, slopes):
    for half, partial_sums in ((0, first), (1, second)):
        span = slice(192 * half, 192 * half + 192)
        hidden = arrived[0, span, :].astype(f32)
        for source in range(1, 8):
            hidden += arrived[source, span, :].astype(f32)
        value, slope = gelu_both(hidden)
        value = value.astype(bf16)
        slopes[span, :] = slope
        for target in range(8):
            payload[8 * half + target, 0:192, :] = partial_sums[192 * target : 192 * target + 192, :]
            payload[8 * half + target, 192:384, :] = value


def slope_kernel(where, arrived, slopes, copies):
    for half in range(2):
        span = slice(192 * half, 192 * half + 192)
        total = arrived[8 * half, 0:192, :].astype(f32)
        for source in range(1, 8):
            total += arrived[8 * half + source, 0:192, :].astype(f32)
        gradient = (total * slopes[span, :]).astype(bf16)
        for target in range(8):
            copies[target, span, :] = gradient


def hidden_rows(gathered, chunk):
    half, source = chunk // 4, 2 * (chunk % 4)
    span = slice(192 * half, 192 * half + 192)
    return jnp.concatenate([gathered[source, span, :], gathered[source + 1, span, :]], axis=0)


def products_kernel(where, arrived, down, cotangents, out, down_grad):
    tokens_of, rows_of = where[0], where[1]
    total = dot(down[0:192, :], arrived[8 * tokens_of, 192:384, :], 0, 0)
    for block in range(1, 8):
        hidden = arrived[8 * tokens_of + block, 192:384, :]
        total += dot(down[192 * block : 192 * block + 192, :], hidden, 0, 0)
    out[...] = total.astype(bf16)
    for block in range(4):
        total = dot(arrived[4 * rows_of + block, 192:384, :], cotangents[0], 1, 1)
        total += dot(arrived[8 + 4 * rows_of + block, 192:384, :], cotangents[1], 1, 1)
        down_grad[192 * block : 192 * block + 192, :] = total.astype(bf16)


def rows_kernel(where, features, gathered, sent, kept):
    rows_of = jnp.concatenate(
        [feature_rows(features, where[0]), feature_rows(features, where[1])], axis=0
    )
    for chunk in range(8):
        rows = hidden_rows(gathered, chunk)
        columns = slice(384 * chunk, 384 * chunk + 384)
        total = dot(rows_of, rows, 1, 1).astype(bf16)
        sent[:, columns] = total[:192]
        kept[:, columns] = total[192:]


def tokens_kernel(where, gathered, w0, w1, w2, w3, own, other, payload):
    total = own[...].astype(f32) + other[...].astype(f32)
    payload[:, 0:96, :] = total.astype(bf16).reshape(8, 96, 256)
    rows = [hidden_rows(gathered, chunk) for chunk in range(8)]
    for b, weights in enumerate((w0, w1, w2, w3)):
        total = dot(weights[:, 0:384], rows[0], 1, 0)
        for chunk in range(1, 8):
            total += dot(weights[:, 384 * chunk : 384 * chunk + 384], rows[chunk], 1, 0)
        payload[pl.ds(2 * where[b], 2), 96:192, :] = total.astype(bf16).reshape(2, 96, 256)


def per_device(tokens, w_up, w_down, grad_out):
    xhi, core = lax.axis_index("xhi"), lax.axis_index("core")
    here = (2 * xhi + core).astype(jnp.int32)
    places = jnp.stack([here, here ^ 1, here ^ 2, here ^ 3])
    far_places = jnp.stack([here ^ 3, here ^ 2])
    near_places = jnp.stack([here ^ 1, here])

    up_across = swap(w_up, "xhi")
    up_beside = swap(w_up, "core")
    up_beyond = swap(up_across, "core")
    up = (w_up, up_beside, up_across, up_beyond)
    both = jnp.concatenate([tokens.T, grad_out.T], axis=0)
    features = exchange(jnp.broadcast_to(both[None], (8, 192, 256)), "inp")
    down = natural(w_down, swap(w_down, "core"), core).reshape(1536, 768)
    g_own = features[:, 96:].reshape(768, 256)
    g_other = swap(g_own, "xhi")

    (hidden_partial,) = local(
        hidden_kernel, [((8, 384, 256), bf16)], 1 << 30, 7 << 20, places, features, *up
    )
    hidden_partial, g_own, g_other = lax.optimization_barrier((hidden_partial, g_own, g_other))
    hidden = exchange(hidden_partial, wgt)
    g = natural(g_own, g_other, xhi)
    payload, slopes = local(
        gelu_kernel,
        [((16, 384, 256), bf16), ((384, 256), f32)],
        1 << 24,
        6 << 20,
        places,
        hidden,
        contract(down, g[0], 1, 0),
        contract(down, g[1], 1, 0),
    )
    arrived = exchange(payload, ("xhi",) + wgt)
    (copies,) = local(
        slope_kernel, [((8, 384, 256), bf16)], 1 << 22, 3 << 20, places, arrived, slopes
    )
    copies, arrived = lax.optimization_barrier((copies, arrived))
    gh = exchange(copies, wgt)

    core_place = jnp.stack([xhi, core]).astype(jnp.int32)
    shapes = [((768, 256), bf16), ((768, 768), bf16)]
    turned = (1 - core_place).astype(jnp.int32)
    out_sent, down_sent = local(products_kernel, shapes, 1 << 20, 1 << 16, turned, arrived, down, g)
    out_other, down_far = swap(out_sent, "xhi"), swap(down_sent, "core")
    out_own, down_near = local(
        products_kernel, shapes, 1 << 20, 1 << 16, core_place, arrived, down, g
    )
    grad_down = (down_near.astype(f32) + down_far.astype(f32)).astype(bf16)
    gh, out_own, grad_down = lax.optimization_barrier((gh, out_own, grad_down))

    row_outs = [((192, 3072), bf16)] * 2
    sent, kept = local(rows_kernel, row_outs, 1 << 29, 4 << 20, far_places, features, gh)
    sent, kept, out_other = lax.optimization_barrier((sent, kept, out_other))
    crossing = (kept.astype(f32) + swap(sent, "core").astype(f32)).astype(bf16)
    (last,) = local(
        tokens_kernel, [((8, 192, 256), bf16)], 1 << 30, 7 << 20, places, gh, *up, out_own, out_other
    )
    last, crossing, gh = lax.optimization_barrier((last, crossing, gh))
    crossed = swap(crossing, "xhi")
    last = exchange(last, "inp")
    sums = jnp.sum(last.astype(f32), axis=0).astype(bf16)
    sent, kept = local(rows_kernel, row_outs, 1 << 29, 4 << 20, near_places, features, gh)
    near = kept.astype(f32) + swap(sent, "core").astype(f32)
    grad_up = (near + crossed.astype(f32)).astype(bf16)
    return (sums[:96].T, sums[96:].T, grad_up, grad_down)


def solution(mesh):
    fine = Mesh(
        np.asarray(mesh.devices).reshape(8, 2, 4, 2, 2), ("inp", "xlo", "y", "xhi", "core")
    )
    out = ("xhi", "core")
    tok = P(out, wgt + ("inp",))
    up = P(wgt + out, "inp")
    down = P(("inp",) + out, wgt)
    return jax.shard_map(
        per_device,
        mesh=fine,
        in_specs=(tok, up, down, tok),
        out_specs=(tok, tok, up, down),
        check_vma=False,
    )
```

time: 252 us -> 206 us (0.82)
  matrix products: 27.3 us -> 1.56 us
  blocking collectives: 23.5 us -> 0 us
  Pallas kernels: 0 us -> 22.8 us
  local copies, waits for them, and re-layouts: 23.7 us -> 9.4 us
  starting transfers between devices: 53.9 us -> 40.8 us
  waiting for transfers between devices: 109 us -> 117 us
    dot_general x8 -> x2, matrix products: 27.3 us -> 1.56 us  [dot(): lax.dot_general(former, latter, (((former_dim,), (latter_dim,)), ((), ())...]
    all_to_all x1 -> x0, blocking collectives: 23.5 us -> none  [exchange(): return lax.all_to_all(value, axis, 0, 0, tiled=True)]
    pallas_call x0 -> x8, Pallas kernels: none -> 22.8 us  [local(): pl.pallas_call(kernel, out_shape=[jax.ShapeDtypeStruct(shape, kind) for s...]
    all_to_all x6 -> x5, waiting for transfers between devices: 52.6 us -> 72.1 us  [exchange(): return lax.all_to_all(value, axis, 0, 0, tiled=True)]
    ppermute x10, waiting for transfers between devices: 56 us -> 45.3 us  [swap(): return lax.ppermute(value, axis, pair)]
    unnamed x40 -> x36, local copies, waits for them, and re-layouts: 15.7 us -> 7.8 us
    ppermute x10, starting transfers between devices: 23.2 us -> 15.9 us  [swap(): return lax.ppermute(value, axis, pair)]
    all_to_all x6 -> x5, starting transfers between devices: 30.8 us -> 24.8 us  [exchange(): return lax.all_to_all(value, axis, 0, 0, tiled=True)]
  transfers between devices with their start and end apart: 16 -> 15, of which waited for: 9 -> 8; matrix products, arithmetic and copies ran while one was open for 21% -> 7% of each run, Pallas kernels for 0% -> 9%
where the time goes in v3:
time: 206 us; the launch traced here: 205 us
  waiting for transfers between devices  117 us (57%)
  starting transfers between devices  40.8 us (20%)
  Pallas kernels  22.8 us (11%)
  other arithmetic  12.4 us (6%)
  local copies, waits for them, and re-layouts  9.4 us (5%)
    all_to_all x5, waiting for transfers between devices, exchange(): return lax.all_to_all(value, axis, 0, 0, tiled=True)  72.1 us
    ppermute x10, waiting for transfers between devices, swap(): return lax.ppermute(value, axis, pair)  45.3 us
    all_to_all x5, starting transfers between devices, exchange(): return lax.all_to_all(value, axis, 0, 0, tiled=True)  24.8 us
    pallas_call x8, Pallas kernels, local(): pl.pallas_call(kernel, out_shape=[jax.ShapeDtypeStruct(shape, kind) for s...  22.8 us
    ppermute x10, starting transfers between devices, swap(): return lax.ppermute(value, axis, pair)  15.9 us
    unnamed x36, local copies, waits for them, and re-layouts  7.8 us
  transfers between devices with their start and end apart: 15, of which 8 were waited for; matrix products, arithmetic and copies ran while one was open for 7% of the time, Pallas kernels for 9%

profile of v3, /device:TPU:1, one launch (start us, length us, event | category | flops | bytes accessed | tf_op | source)
XLA Modules:
  0.0 205.2 jit_solution(14641878084080414908)
XLA Ops:
  0.6 3.7 %collective-permute-start.1 = (bf16[192,3072]{1,0:T(8,128)(2,1)}, bf16[192,3072]{1,0:T(8,128)(2,1)S(1)}, u32[]{:S(2)}, u32[]{:S(2)}) collective-permute-start(bf16[192,3072]{1,0:T(8,128)(2,1)} %w0.3), channel_id=1, source_target_pairs={{0,2},{2,0},{1,3},{3,1},{4,6},{6,4},{5,7},{7,5},{8,10},{10,8},{9,1... | collective-permute-start | bytes 3538952 | tf_op jit(solution)/shard_map/ppermute | solution.py:39
  4.3 0.8 pad_maximum_fusion
  5.1 0.9 broadcast_in_dim.2
  6.1 8.2 %all-to-all-start = ((bf16[8,192,256]{2,1,0:T(8,128)(2,1)}), bf16[8,192,256]{2,1,0:T(8,128)(2,1)S(1)}, u32[]{:S(2)}, u32[]{:S(2)}) async-start(bf16[8,192,256]{2,1,0:T(8,128)(2,1)} %broadcast_in_dim.2), calls=%async_computation | async-start | bytes 1572864 | tf_op jit(solution)/shard_map/all_to_all | solution.py:43
  14.3 1.3 collective-permute-start
  15.6 13.7 %collective-permute-done.1.w2 = bf16[192,3072]{1,0:T(8,128)(2,1)S(1)} collective-permute-done((bf16[192,3072]{1,0:T(8,128)(2,1)}, bf16[192,3072]{1,0:T(8,128)(2,1)S(1)}, u32[]{:S(2)}, u32[]{:S(2)}) %collective-permute-start.1) | collective-permute-done | bytes 1179680 | tf_op jit(solution)/shard_map/ppermute | solution.py:39
  29.3 2.2 %collective-permute-start.2 = (bf16[192,3072]{1,0:T(8,128)(2,1)S(1)}, bf16[192,3072]{1,0:T(8,128)(2,1)}, u32[]{:S(2)}, u32[]{:S(2)}) collective-permute-start(bf16[192,3072]{1,0:T(8,128)(2,1)S(1)} %collective-permute-done.1.w2), channel_id=1, source_target_pairs={{0,1},{1,0},{2,3},{3,2},{4,5},{5,4},{6,7},{7,6},{8,9},{9,8},{10,11... | collective-permute-start | bytes 3538952 | tf_op jit(solution)/shard_map/ppermute | solution.py:39
  31.4 6.4 %all-to-all-done.features = bf16[8,192,256]{2,1,0:T(8,128)(2,1)S(1)} async-done(((bf16[8,192,256]{2,1,0:T(8,128)(2,1)}), bf16[8,192,256]{2,1,0:T(8,128)(2,1)S(1)}, u32[]{:S(2)}, u32[]{:S(2)}) %all-to-all-start) | async-done | bytes 786464 | tf_op jit(solution)/shard_map/all_to_all | solution.py:43
  37.9 0.3 collective-permute-start.3
  38.3 5.3 %shard_map.75 = bf16[8,384,256]{2,1,0:T(8,128)(2,1)} custom-call(s32[4]{0:T(128)S(1)} %pad_add_fusion.where, bf16[8,192,256]{2,1,0:T(8,128)(2,1)S(1)} %all-to-all-done.features, bf16[192,3072]{1,0:T(8,128)(2,1)S(1)} %copy-done.9, bf16[192,3072]{1,0:T(8,128)(2,1)} %collective-permute-done.w1, bf16[192,3072]{1,0:T(8,128)(2,1)S(1)} %collective-permute-done.1.w2, ...), custom_call_target="tpu_custom_call" | custom-call | flops 1073741824 | bytes 7340032 | tf_op jit(solution)/shard_map/pallas_call | solution.py:52
  43.6 6.2 %collective-permute-done.3 = bf16[768,256]{1,0:T(8,128)(2,1)} collective-permute-done((bf16[768,256]{1,0:T(8,128)(2,1)S(1)}, bf16[768,256]{1,0:T(8,128)(2,1)}, u32[]{:S(2)}, u32[]{:S(2)}) %collective-permute-start.3) | collective-permute-done | bytes 393248 | tf_op jit(solution)/shard_map/ppermute | solution.py:39
  49.7 4.4 %all-to-all-start.1 = ((bf16[8,384,256]{2,1,0:T(8,128)(2,1)}), bf16[8,384,256]{2,1,0:T(8,128)(2,1)S(1)}, u32[]{:S(2)}, u32[]{:S(2)}) async-start(bf16[8,384,256]{2,1,0:T(8,128)(2,1)} %shard_map.75), calls=%async_computation.1 | async-start | bytes 3145728 | tf_op jit(solution)/shard_map/all_to_all | solution.py:43
  54.1 2.0 maximum_select_fusion
  56.2 1.8 maximum_select_fusion.1.cotangents
  58.0 0.8 convolution_convert_fusion.second
  58.9 0.8 convolution_convert_fusion.1.first
  59.7 15.0 %all-to-all-done.1.arrived = bf16[8,384,256]{2,1,0:T(8,128)(2,1)S(1)} async-done(((bf16[8,384,256]{2,1,0:T(8,128)(2,1)}), bf16[8,384,256]{2,1,0:T(8,128)(2,1)S(1)}, u32[]{:S(2)}, u32[]{:S(2)}) %all-to-all-start.1) | async-done | bytes 1572896 | tf_op jit(solution)/shard_map/all_to_all | solution.py:43
  74.6 1.0 shard_map.76
  75.7 1.6 copy-done.13
  77.3 4.4 %all-to-all-start.2 = ((bf16[16,384,256]{2,1,0:T(8,128)(2,1)}), bf16[16,384,256]{2,1,0:T(8,128)(2,1)S(1)}, u32[]{:S(2)}, u32[]{:S(2)}) async-start(bf16[16,384,256]{2,1,0:T(8,128)(2,1)} %copy-done.13), calls=%async_computation.2 | async-start | bytes 6291456 | tf_op jit(solution)/shard_map/all_to_all | solution.py:43
  81.8 40.4 %all-to-all-done.2.arrived = bf16[16,384,256]{2,1,0:T(8,128)(2,1)S(1)} async-done(((bf16[16,384,256]{2,1,0:T(8,128)(2,1)}), bf16[16,384,256]{2,1,0:T(8,128)(2,1)S(1)}, u32[]{:S(2)}, u32[]{:S(2)}) %all-to-all-start.2) | async-done | bytes 3145760 | tf_op jit(solution)/shard_map/all_to_all | solution.py:43
  122.2 0.8 shard_map.77
  122.9 1.2 copy-done.8
  124.1 0.3 copy-done.6
  124.4 3.5 %shard_map.79 = (bf16[768,256]{1,0:T(8,128)(2,1)S(1)}, bf16[768,768]{1,0:T(8,128)(2,1)}) custom-call(s32[2]{0:T(128)S(1)} %get-tuple-element.52.where, bf16[16,384,256]{2,1,0:T(8,128)(2,1)S(1)} %all-to-all-done.2.arrived, bf16[1536,768]{1,0:T(8,128)(2,1)S(1)} %bitcast.28, bf16[2,768,256]{2,1,0:T(8,128)(2,1)S(1)} %copy-done.6), custom_call_target="tpu_custom_call" | custom-call | flops 1048576 | bytes 65536 | tf_op jit(solution)/shard_map/pallas_call | solution.py:52
  127.9 3.5 %collective-permute-start.5 = (bf16[768,768]{1,0:T(8,128)(2,1)}, bf16[768,768]{1,0:T(8,128)(2,1)}, u32[]{:S(2)}, u32[]{:S(2)}) collective-permute-start(bf16[768,768]{1,0:T(8,128)(2,1)} %get-tuple-element.37), channel_id=1, source_target_pairs={{0,1},{1,0},{2,3},{3,2},{4,5},{5,4},{6,7},{7,6},{8,9},{9,8},{10,11... | collective-permute-start | bytes 3538952 | tf_op jit(solution)/shard_map/ppermute | solution.py:39
  131.4 4.3 %all-to-all-start.3 = ((bf16[8,384,256]{2,1,0:T(8,128)(2,1)}), bf16[8,384,256]{2,1,0:T(8,128)(2,1)}, u32[]{:S(2)}, u32[]{:S(2)}) async-start(bf16[8,384,256]{2,1,0:T(8,128)(2,1)} %copy-done.8), calls=%async_computation.3 | async-start | bytes 3145728 | tf_op jit(solution)/shard_map/all_to_all | solution.py:43
  135.7 1.4 collective-permute-start.6
  137.2 1.7 copy-done.2
  138.8 1.1 copy-done.7
  140.0 2.5 %shard_map.78 = (bf16[768,256]{1,0:T(8,128)(2,1)S(1)}, bf16[768,768]{1,0:T(8,128)(2,1)S(1)}) custom-call(s32[2]{0:T(128)S(1)} %get-tuple-element.53.where, bf16[16,384,256]{2,1,0:T(8,128)(2,1)S(1)} %all-to-all-done.2.arrived, bf16[1536,768]{1,0:T(8,128)(2,1)S(1)} %bitcast.29, bf16[2,768,256]{2,1,0:T(8,128)(2,1)S(1)} %copy-done.7), custom_call_target="tpu_custom_call" | custom-call | flops 1048576 | bytes 65536 | tf_op jit(solution)/shard_map/pallas_call | solution.py:52
  142.5 0.8 copy-done.14
  143.3 2.6 %add_convert_fusion.2 = bf16[768,768]{1,0:T(8,128)(2,1)} fusion(bf16[768,768]{1,0:T(8,128)(2,1)} %collective-permute-done.5, bf16[768,768]{1,0:T(8,128)(2,1)S(1)} %get-tuple-element.36), kind=kLoop, calls=%fused_computation.5 | loop fusion | flops 2359296 | bytes 3538944 | tf_op jit(solution)/shard_map/convert_element_type | solution.py:195
  145.9 10.4 %all-to-all-done.3.gathered = bf16[8,384,256]{2,1,0:T(8,128)(2,1)} async-done(((bf16[8,384,256]{2,1,0:T(8,128)(2,1)}), bf16[8,384,256]{2,1,0:T(8,128)(2,1)}, u32[]{:S(2)}, u32[]{:S(2)}) %all-to-all-start.3) | async-done | bytes 1572896 | tf_op jit(solution)/shard_map/all_to_all | solution.py:43
  156.3 2.4 %shard_map.80 = (bf16[192,3072]{1,0:T(8,128)(2,1)S(1)}, bf16[192,3072]{1,0:T(8,128)(2,1)S(1)}) custom-call(s32[2]{0:T(128)S(1)} %pad_add_fusion.2.where, bf16[8,192,256]{2,1,0:T(8,128)(2,1)S(1)} %copy-done.4, bf16[8,384,256]{2,1,0:T(8,128)(2,1)} %all-to-all-done.3.gathered), custom_call_target="tpu_custom_call" | custom-call | flops 536870912 | bytes 4194304 | tf_op jit(solution)/shard_map/pallas_call | solution.py:52
  158.7 4.0 %collective-permute-done.6.other = bf16[768,256]{1,0:T(8,128)(2,1)S(1)} collective-permute-done((bf16[768,256]{1,0:T(8,128)(2,1)}, bf16[768,256]{1,0:T(8,128)(2,1)S(1)}, u32[]{:S(2)}, u32[]{:S(2)}) %collective-permute-start.6) | collective-permute-done | bytes 393248 | tf_op jit(solution)/shard_map/ppermute | solution.py:39
  162.7 1.6 collective-permute-start.7
  164.4 1.0 copy-done.15
  165.4 4.9 %shard_map.81 = bf16[8,192,256]{2,1,0:T(8,128)(2,1)} custom-call(s32[4]{0:T(128)S(1)} %pad_add_fusion.where, bf16[8,384,256]{2,1,0:T(8,128)(2,1)} %all-to-all-done.3.gathered, bf16[192,3072]{1,0:T(8,128)(2,1)S(1)} %copy-done.10, bf16[192,3072]{1,0:T(8,128)(2,1)} %collective-permute-done.w1, bf16[192,3072]{1,0:T(8,128)(2,1)S(1)} %copy-done.12, ...), custom_call_target="tpu_custom_call" | custom-call | flops 1073741824 | bytes 7340032 | tf_op jit(solution)/shard_map/pallas_call | solution.py:52
  170.3 1.4 add_convert_fusion.1
  171.8 1.5 collective-permute-start.9
  173.3 2.4 %shard_map.82 = (bf16[192,3072]{1,0:T(8,128)(2,1)S(1)}, bf16[192,3072]{1,0:T(8,128)(2,1)S(1)}) custom-call(s32[2]{0:T(128)S(1)} %pad_add_fusion.3.where, bf16[8,192,256]{2,1,0:T(8,128)(2,1)S(1)} %copy-done.4, bf16[8,384,256]{2,1,0:T(8,128)(2,1)} %all-to-all-done.3.gathered), custom_call_target="tpu_custom_call" | custom-call | flops 536870912 | bytes 4194304 | tf_op jit(solution)/shard_map/pallas_call | solution.py:52
  175.7 0.4 collective-permute-start.8
  176.1 3.6 %all-to-all-start.4 = ((bf16[8,192,256]{2,1,0:T(8,128)(2,1)}), bf16[8,192,256]{2,1,0:T(8,128)(2,1)S(1)}, u32[]{:S(2)}, u32[]{:S(2)}) async-start(bf16[8,192,256]{2,1,0:T(8,128)(2,1)} %shard_map.81), calls=%async_computation.4 | async-start | bytes 1572864 | tf_op jit(solution)/shard_map/all_to_all | solution.py:43
  179.7 21.4 %collective-permute-done.9 = bf16[192,3072]{1,0:T(8,128)(2,1)} collective-permute-done((bf16[192,3072]{1,0:T(8,128)(2,1)}, bf16[192,3072]{1,0:T(8,128)(2,1)}, u32[]{:S(2)}, u32[]{:S(2)}) %collective-permute-start.9) | collective-permute-done | bytes 1179680 | tf_op jit(solution)/shard_map/ppermute | solution.py:39
  201.2 3.2 %add_convert_fusion = bf16[192,3072]{1,0:T(8,128)(2,1)} fusion(bf16[192,3072]{1,0:T(8,128)(2,1)} %collective-permute-done.9, bf16[192,3072]{1,0:T(8,128)(2,1)} %collective-permute-done.8, bf16[192,3072]{1,0:T(8,128)(2,1)S(1)} %get-tuple-element.48), kind=kLoop, calls=%fused_computation.3 | loop fusion | flops 3538944 | bytes 4718592 | tf_op jit(solution)/shard_map/convert_element_type | solution.py:211
  204.4 0.1 reduce_sum.12
  204.5 0.6 slice_bitcast_fusion.4
  (42 shorter events, 0.5 us)
Async XLA Ops:
  0.6 13.6 %copy-start.9 = (bf16[192,3072]{1,0:T(8,128)(2,1)S(1)}, bf16[192,3072]{1,0:T(8,128)(2,1)}, u32[]{:S(2)}) copy-start(bf16[192,3072]{1,0:T(8,128)(2,1)} %w0.3) | copy-start | bytes 3538948
  0.6 28.6 %collective-permute-start.1 = (bf16[192,3072]{1,0:T(8,128)(2,1)}, bf16[192,3072]{1,0:T(8,128)(2,1)S(1)}, u32[]{:S(2)}, u32[]{:S(2)}) collective-permute-start(bf16[192,3072]{1,0:T(8,128)(2,1)} %w0.3), channel_id=1, source_target_pairs={{0,2},{2,0},{1,3},{3,1},{4,6},{6,4},{5,7},{7,5},{8,10},{10,8},{9,1... | collective-permute-start | bytes 3538952 | tf_op jit(solution)/shard_map/ppermute | solution.py:39
  6.1 31.8 %all-to-all-start = ((bf16[8,192,256]{2,1,0:T(8,128)(2,1)}), bf16[8,192,256]{2,1,0:T(8,128)(2,1)S(1)}, u32[]{:S(2)}, u32[]{:S(2)}) async-start(bf16[8,192,256]{2,1,0:T(8,128)(2,1)} %broadcast_in_dim.2), calls=%async_computation | async-start | bytes 1572864 | tf_op jit(solution)/shard_map/all_to_all | solution.py:43
  14.3 24.0 %collective-permute-start = (bf16[192,3072]{1,0:T(8,128)(2,1)S(1)}, bf16[192,3072]{1,0:T(8,128)(2,1)}, u32[]{:S(2)}, u32[]{:S(2)}) collective-permute-start(bf16[192,3072]{1,0:T(8,128)(2,1)S(1)} %copy-done.9), channel_id=1, source_target_pairs={{0,1},{1,0},{2,3},{3,2},{4,5},{5,4},{6,7},{7,6},{8,9},{9,8},{10,11... | collective-permute-start | bytes 3538952 | tf_op jit(solution)/shard_map/ppermute | solution.py:39
  29.3 14.3 %copy-start.11 = (bf16[192,3072]{1,0:T(8,128)(2,1)}, bf16[192,3072]{1,0:T(8,128)(2,1)S(1)}, u32[]{:S(2)}) copy-start(bf16[192,3072]{1,0:T(8,128)(2,1)S(1)} %collective-permute-done.1.w2) | copy-start | bytes 3538948
  29.3 9.0 %collective-permute-start.2 = (bf16[192,3072]{1,0:T(8,128)(2,1)S(1)}, bf16[192,3072]{1,0:T(8,128)(2,1)}, u32[]{:S(2)}, u32[]{:S(2)}) collective-permute-start(bf16[192,3072]{1,0:T(8,128)(2,1)S(1)} %collective-permute-done.1.w2), channel_id=1, source_target_pairs={{0,1},{1,0},{2,3},{3,2},{4,5},{5,4},{6,7},{7,6},{8,9},{9,8},{10,11... | collective-permute-start | bytes 3538952 | tf_op jit(solution)/shard_map/ppermute | solution.py:39
  31.4 22.7 %collective-permute-start.4 = (bf16[768,768]{1,0:T(8,128)(2,1)}, bf16[768,768]{1,0:T(8,128)(2,1)}, u32[]{:S(2)}, u32[]{:S(2)}) collective-permute-start(bf16[768,768]{1,0:T(8,128)(2,1)} %param.6), channel_id=1, source_target_pairs={{0,1},{1,0},{2,3},{3,2},{4,5},{5,4},{6,7},{7,6},{8,9},{9,8},{10,11... | collective-permute-start | bytes 3538952 | tf_op jit(solution)/shard_map/ppermute | solution.py:39
  37.8 5.7 %copy-start.3 = (bf16[8,192,256]{2,1,0:T(8,128)(2,1)}, bf16[8,192,256]{2,1,0:T(8,128)(2,1)S(1)}, u32[]{:S(2)}) copy-start(bf16[8,192,256]{2,1,0:T(8,128)(2,1)S(1)} %all-to-all-done.features) | copy-start | bytes 2359300
  37.9 11.9 %collective-permute-start.3 = (bf16[768,256]{1,0:T(8,128)(2,1)S(1)}, bf16[768,256]{1,0:T(8,128)(2,1)}, u32[]{:S(2)}, u32[]{:S(2)}) collective-permute-start(bf16[768,256]{1,0:T(8,128)(2,1)S(1)} %bitcast.30), channel_id=1, source_target_pairs={{0,2},{2,0},{1,3},{3,1},{4,6},{6,4},{5,7},{7,5},{8,10},{10,8},{9,1... | collective-permute-start | bytes 1179656 | tf_op jit(solution)/shard_map/ppermute | solution.py:39
  49.7 4.4 %copy-start.17 = (bf16[768,768]{1,0:T(8,128)(2,1)S(1)}, bf16[768,768]{1,0:T(8,128)(2,1)}, u32[]{:S(2)}) copy-start(bf16[768,768]{1,0:T(8,128)(2,1)} %param.6) | copy-start | bytes 3538948
  49.7 24.9 %all-to-all-start.1 = ((bf16[8,384,256]{2,1,0:T(8,128)(2,1)}), bf16[8,384,256]{2,1,0:T(8,128)(2,1)S(1)}, u32[]{:S(2)}, u32[]{:S(2)}) async-start(bf16[8,384,256]{2,1,0:T(8,128)(2,1)} %shard_map.75), calls=%async_computation.1 | async-start | bytes 3145728 | tf_op jit(solution)/shard_map/all_to_all | solution.py:43
  56.2 2.6 %copy-start = (bf16[2,768,768]{2,1,0:T(8,128)(2,1)}, bf16[2,768,768]{2,1,0:T(8,128)(2,1)S(1)}, u32[]{:S(2)}) copy-start(bf16[2,768,768]{2,1,0:T(8,128)(2,1)S(1)} %maximum_select_fusion) | copy-start | bytes 7077892
  58.0 0.9 copy-start.5
  75.7 1.6 copy-start.13
  77.3 44.9 %all-to-all-start.2 = ((bf16[16,384,256]{2,1,0:T(8,128)(2,1)}), bf16[16,384,256]{2,1,0:T(8,128)(2,1)S(1)}, u32[]{:S(2)}, u32[]{:S(2)}) async-start(bf16[16,384,256]{2,1,0:T(8,128)(2,1)} %copy-done.13), calls=%async_computation.2 | async-start | bytes 6291456 | tf_op jit(solution)/shard_map/all_to_all | solution.py:43
  122.2 1.9 copy-start.1
  122.2 2.2 %copy-start.6 = (bf16[2,768,256]{2,1,0:T(8,128)(2,1)S(1)}, bf16[2,768,256]{2,1,0:T(8,128)(2,1)}, u32[]{:S(2)}) copy-start(bf16[2,768,256]{2,1,0:T(8,128)(2,1)} %copy-done.5) | copy-start | bytes 2359300
  122.9 1.2 copy-start.8
  127.9 3.5 %copy-start.16 = (bf16[768,256]{1,0:T(8,128)(2,1)}, bf16[768,256]{1,0:T(8,128)(2,1)S(1)}, u32[]{:S(2)}) copy-start(bf16[768,256]{1,0:T(8,128)(2,1)S(1)} %get-tuple-element.42) | copy-start | bytes 1179652
  127.9 15.3 %collective-permute-start.5 = (bf16[768,768]{1,0:T(8,128)(2,1)}, bf16[768,768]{1,0:T(8,128)(2,1)}, u32[]{:S(2)}, u32[]{:S(2)}) collective-permute-start(bf16[768,768]{1,0:T(8,128)(2,1)} %get-tuple-element.37), channel_id=1, source_target_pairs={{0,1},{1,0},{2,3},{3,2},{4,5},{5,4},{6,7},{7,6},{8,9},{9,8},{10,11... | collective-permute-start | bytes 3538952 | tf_op jit(solution)/shard_map/ppermute | solution.py:39
  131.4 24.9 %all-to-all-start.3 = ((bf16[8,384,256]{2,1,0:T(8,128)(2,1)}), bf16[8,384,256]{2,1,0:T(8,128)(2,1)}, u32[]{:S(2)}, u32[]{:S(2)}) async-start(bf16[8,384,256]{2,1,0:T(8,128)(2,1)} %copy-done.8), calls=%async_computation.3 | async-start | bytes 3145728 | tf_op jit(solution)/shard_map/all_to_all | solution.py:43
  135.7 27.0 %collective-permute-start.6 = (bf16[768,256]{1,0:T(8,128)(2,1)}, bf16[768,256]{1,0:T(8,128)(2,1)S(1)}, u32[]{:S(2)}, u32[]{:S(2)}) collective-permute-start(bf16[768,256]{1,0:T(8,128)(2,1)} %copy-done.16), channel_id=1, source_target_pairs={{0,2},{2,0},{1,3},{3,1},{4,6},{6,4},{5,7},{7,5},{8,10},{10,8},{9,1... | collective-permute-start | bytes 1179656 | tf_op jit(solution)/shard_map/ppermute | solution.py:39
  137.2 1.7 copy-start.2
  138.8 1.1 copy-start.7
  142.5 0.8 copy-start.14
  143.2 13.0 %copy-start.4 = (bf16[8,192,256]{2,1,0:T(8,128)(2,1)S(1)}, bf16[8,192,256]{2,1,0:T(8,128)(2,1)}, u32[]{:S(2)}) copy-start(bf16[8,192,256]{2,1,0:T(8,128)(2,1)} %copy-done.3) | copy-start | bytes 2359300
  145.9 18.5 %copy-start.10 = (bf16[192,3072]{1,0:T(8,128)(2,1)S(1)}, bf16[192,3072]{1,0:T(8,128)(2,1)}, u32[]{:S(2)}) copy-start(bf16[192,3072]{1,0:T(8,128)(2,1)} %w0.3) | copy-start | bytes 3538948
  145.9 18.5 %copy-start.12 = (bf16[192,3072]{1,0:T(8,128)(2,1)S(1)}, bf16[192,3072]{1,0:T(8,128)(2,1)}, u32[]{:S(2)}) copy-start(bf16[192,3072]{1,0:T(8,128)(2,1)} %copy-done.11) | copy-start | bytes 3538948
  162.7 7.6 %collective-permute-start.7 = (bf16[192,3072]{1,0:T(8,128)(2,1)S(1)}, bf16[192,3072]{1,0:T(8,128)(2,1)S(1)}, u32[]{:S(2)}, u32[]{:S(2)}) collective-permute-start(bf16[192,3072]{1,0:T(8,128)(2,1)S(1)} %get-tuple-element.45), channel_id=1, source_target_pairs={{0,1},{1,0},{2,3},{3,2},{4,5},{5,4},{6,7},{7,6},{8,9},{9,8},{10,11... | collective-permute-start | bytes 3538952 | tf_op jit(solution)/shard_map/ppermute | solution.py:39
  164.4 1.0 copy-start.15
  171.8 29.4 %collective-permute-start.9 = (bf16[192,3072]{1,0:T(8,128)(2,1)}, bf16[192,3072]{1,0:T(8,128)(2,1)}, u32[]{:S(2)}, u32[]{:S(2)}) collective-permute-start(bf16[192,3072]{1,0:T(8,128)(2,1)} %add_convert_fusion.1), channel_id=1, source_target_pairs={{0,2},{2,0},{1,3},{3,1},{4,6},{6,4},{5,7},{7,5},{8,10},{10,8},{9,1... | collective-permute-start | bytes 3538952 | tf_op jit(solution)/shard_map/ppermute | solution.py:39
  175.7 25.5 %collective-permute-start.8 = (bf16[192,3072]{1,0:T(8,128)(2,1)S(1)}, bf16[192,3072]{1,0:T(8,128)(2,1)}, u32[]{:S(2)}, u32[]{:S(2)}) collective-permute-start(bf16[192,3072]{1,0:T(8,128)(2,1)S(1)} %get-tuple-element.49), channel_id=1, source_target_pairs={{0,1},{1,0},{2,3},{3,2},{4,5},{5,4},{6,7},{7,6},{8,9},{9,8},{10,11... | collective-permute-start | bytes 3538952 | tf_op jit(solution)/shard_map/ppermute | solution.py:39
  176.1 28.3 %all-to-all-start.4 = ((bf16[8,192,256]{2,1,0:T(8,128)(2,1)}), bf16[8,192,256]{2,1,0:T(8,128)(2,1)S(1)}, u32[]{:S(2)}, u32[]{:S(2)}) async-start(bf16[8,192,256]{2,1,0:T(8,128)(2,1)} %shard_map.81), calls=%async_computation.4 | async-start | bytes 1572864 | tf_op jit(solution)/shard_map/all_to_all | solution.py:43

commit v4 on v3

v4 whole, which is shorter than its diff:
```python
import jax
import jax.numpy as jnp
import numpy as np
from jax import lax
from jax.experimental import pallas as pl
from jax.experimental.pallas import tpu as pltpu
from jax.sharding import Mesh, PartitionSpec as P

tanh_scale = 0.7978845608028654
cubic_weight = 0.044715
pair = [(0, 1), (1, 0)]
wgt = ("xlo", "y")
bf16, f32 = jnp.bfloat16, jnp.float32


def gelu_both(hidden):
    tangent = jnp.tanh(tanh_scale * (hidden + cubic_weight * hidden * hidden * hidden))
    value = 0.5 * hidden * (1.0 + tangent)
    slope = 0.5 * (1.0 + tangent) + 0.5 * hidden * (1.0 - tangent * tangent) * tanh_scale * (
        1.0 + 3.0 * cubic_weight * hidden * hidden
    )
    return value, slope


def dot(former, latter, former_dim, latter_dim):
    return lax.dot_general(
        former,
        latter,
        (((former_dim,), (latter_dim,)), ((), ())),
        preferred_element_type=f32,
    )


def swap(value, axis):
    return lax.ppermute(value, axis, pair)


def exchange(value, axis):
    return lax.all_to_all(value, axis, 0, 0, tiled=True)


def natural(own, other, place):
    return jnp.where(place == 0, jnp.stack([own, other]), jnp.stack([other, own]))


def local(kernel, outs, *operands, kinds=None, flops=1 << 20):
    whole = pl.BlockSpec(memory_space=pltpu.VMEM)
    kinds = kinds or [bf16] * len(outs)
    return pl.pallas_call(
        kernel,
        out_shape=[jax.ShapeDtypeStruct(shape, kind) for shape, kind in zip(outs, kinds)],
        in_specs=[pl.BlockSpec(memory_space=pltpu.SMEM)] + [whole] * (len(operands) - 1),
        out_specs=[whole] * len(outs),
        compiler_params=pltpu.CompilerParams(vmem_limit_bytes=16 * 1024 * 1024),
        cost_estimate=pl.CostEstimate(flops=flops, bytes_accessed=1 << 16, transcendentals=0),
    )(*operands)


def feature_rows(features, block):
    return features[pl.ds(2 * block, 2), 0:96, :].reshape(192, 256)


def hidden_kernel(where, features, w0, w1, w2, w3, out):
    turned = [feature_rows(features, where[b]).T for b in range(4)]
    for chunk in range(8):
        columns = slice(384 * chunk, 384 * chunk + 384)
        total = dot(turned[0], w0[:, columns], 1, 0)
        for b, weights in ((1, w1), (2, w2), (3, w3)):
            total += dot(turned[b], weights[:, columns], 1, 0)
        rows = total.astype(bf16).T
        half, target = chunk // 4, 2 * (chunk % 4)
        span = slice(192 * half, 192 * half + 192)
        out[target, span, :] = rows[:192]
        out[target + 1, span, :] = rows[192:]


def partial_kernel(where, down, own, other, partial_sums):
    for side, cotangents in ((where[0], own), (1 - where[0], other)):
        for block in range(8):
            rows = down[192 * block : 192 * block + 192, :]
            partial_sums[side, block] = dot(rows, cotangents[...], 1, 0).astype(bf16)


def gelu_kernel(where, arrived, values, slopes):
    for half in range(2):
        span = slice(192 * half, 192 * half + 192)
        hidden = arrived[0, span, :].astype(f32)
        for source in range(1, 8):
            hidden += arrived[source, span, :].astype(f32)
        value, slope = gelu_both(hidden)
        values[half] = value.astype(bf16)
        slopes[span, :] = slope


def output_kernel(where, gathered, down, own, sent):
    for result, first in ((sent, 576), (own, 384)):
        total = dot(down[0:192, :], gathered[0, first : first + 192, :], 0, 0)
        for block in range(1, 8):
            hidden = gathered[block, first : first + 192, :]
            total += dot(down[192 * block : 192 * block + 192, :], hidden, 0, 0)
        result[...] = total.astype(bf16)


def down_kernel(where, gathered, own, other, sent, kept):
    for result, rows_of in ((sent, 1 - where[1]), (kept, where[1])):
        for block in range(4):
            place = 4 * rows_of + block
            total = dot(gathered[place, 384:576, :], own[...], 1, 1)
            total += dot(gathered[place, 576:768, :], other[...], 1, 1)
            result[192 * block : 192 * block + 192, :] = total.astype(bf16)


def hidden_rows(gathered, chunk):
    half, source = chunk // 4, 2 * (chunk % 4)
    span = slice(192 * half, 192 * half + 192)
    return jnp.concatenate([gathered[source, span, :], gathered[source + 1, span, :]], axis=0)


def rows_kernel(where, features, gathered, sent, kept):
    rows_of = jnp.concatenate(
        [feature_rows(features, where[0]), feature_rows(features, where[1])], axis=0
    )
    for chunk in range(8):
        rows = hidden_rows(gathered, chunk)
        columns = slice(384 * chunk, 384 * chunk + 384)
        total = dot(rows_of, rows, 1, 1).astype(bf16)
        sent[:, columns] = total[:192]
        kept[:, columns] = total[192:]


def tokens_kernel(where, gathered, w0, w1, w2, w3, payload):
    total = None
    for chunk in range(4):
        columns = slice(768 * chunk, 768 * chunk + 768)
        rows = jnp.concatenate(
            [hidden_rows(gathered, 2 * chunk), hidden_rows(gathered, 2 * chunk + 1)], axis=0
        )
        weights = jnp.concatenate([w[:, columns] for w in (w0, w1, w2, w3)], axis=0)
        term = dot(weights, rows, 1, 0)
        total = term if total is None else total + term
    for b in range(4):
        block = total[192 * b : 192 * b + 192].astype(bf16).reshape(2, 96, 256)
        payload[pl.ds(2 * where[b], 2), 96:192, :] = block
    payload[:, 0:96, :] = jnp.zeros((8, 96, 256), bf16)


def finish_kernel(where, own, other, given, payload):
    total = own[...].astype(f32) + other[...].astype(f32)
    payload[:, 0:96, :] = total.astype(bf16).reshape(8, 96, 256)
    payload[:, 96:192, :] = given[:, 96:192, :]


def per_device(tokens, w_up, w_down, grad_out):
    xhi, core = lax.axis_index("xhi"), lax.axis_index("core")
    here = (2 * xhi + core).astype(jnp.int32)
    places = jnp.stack([here, here ^ 1, here ^ 2, here ^ 3])
    far_places = jnp.stack([here ^ 3, here ^ 2])
    near_places = jnp.stack([here ^ 1, here])
    sides = jnp.stack([xhi, core, xhi]).astype(jnp.int32)
    far_sides = jnp.stack([1 - xhi, 1 - core, xhi]).astype(jnp.int32)

    up_across = swap(w_up, "xhi")
    up_beside = swap(w_up, "core")
    up_beyond = swap(up_across, "core")
    up = (w_up, up_beside, up_across, up_beyond)
    both = jnp.concatenate([tokens.T, grad_out.T], axis=0)
    features = exchange(jnp.broadcast_to(both[None], (8, 192, 256)), "inp")
    down = natural(w_down, swap(w_down, "core"), core).reshape(1536, 768)
    g_own = features[:, 96:].reshape(768, 256)
    g_other = swap(g_own, "xhi")

    (hidden_partial,) = local(
        hidden_kernel, [(8, 384, 256)], places, features, *up, flops=4 << 30
    )
    hidden_partial, g_other = lax.optimization_barrier((hidden_partial, g_other))
    hidden = exchange(hidden_partial, wgt)
    (partial_sums,) = local(partial_kernel, [(2, 8, 192, 256)], sides, down, g_own, g_other)
    partial_sums, hidden = lax.optimization_barrier((partial_sums, hidden))
    arrived = exchange(partial_sums.reshape(16, 192, 256), ("xhi",) + wgt)
    values, slopes = local(
        gelu_kernel, [(2, 192, 256), (384, 256)], places, hidden, kinds=[bf16, f32]
    )
    crossing = swap(lax.dynamic_index_in_dim(values, 1 - xhi, 0, keepdims=False), "xhi")
    act_own = lax.dynamic_index_in_dim(values, xhi, 0, keepdims=False)
    acts = lax.optimization_barrier(jnp.concatenate([act_own, crossing], axis=0))
    grad_act = jnp.sum(arrived.reshape(2, 8, 192, 256).astype(f32), axis=1)
    grad_hidden = (grad_act * slopes.reshape(2, 192, 256)).astype(bf16).reshape(384, 256)
    portion = jnp.concatenate([grad_hidden, acts], axis=0)
    gathered = exchange(jnp.broadcast_to(portion[None], (8, 768, 256)), wgt)

    out_own, out_sent = local(output_kernel, [(768, 256)] * 2, sides, gathered, down)
    out_other = swap(out_sent, "xhi")
    gathered, out_sent = lax.optimization_barrier((gathered, out_sent))
    row_outs = [(192, 3072)] * 2
    sent, kept = local(rows_kernel, row_outs, far_places, features, gathered)
    gathered, sent, kept = lax.optimization_barrier((gathered, sent, kept))
    beyond = swap(sent, "core")
    (last,) = local(tokens_kernel, [(8, 192, 256)], places, gathered, *up, flops=4 << 30)
    near_sent, near_kept = local(
        rows_kernel, row_outs, near_places, features, gathered, flops=4 << 30
    )
    crossing = (kept.astype(f32) + beyond.astype(f32)).astype(bf16)
    last, crossing, gathered, near_sent, near_kept = lax.optimization_barrier(
        (last, crossing, gathered, near_sent, near_kept)
    )
    crossed = swap(crossing, "xhi")
    (last,) = local(finish_kernel, [(8, 192, 256)], places, out_own, out_other, last)
    last = exchange(last, "inp")
    sums = jnp.sum(last.astype(f32), axis=0).astype(bf16)
    near = near_kept.astype(f32) + swap(near_sent, "core").astype(f32)
    grad_up = (lax.optimization_barrier(near) + crossed.astype(f32)).astype(bf16)
    down_sent, down_kept = local(
        down_kernel, [(768, 768)] * 2, sides, gathered, g_own, g_other, flops=4 << 30
    )
    grad_down = (down_kept.astype(f32) + swap(down_sent, "core").astype(f32)).astype(bf16)
    return (sums[:96].T, sums[96:].T, grad_up, grad_down)


def solution(mesh):
    fine = Mesh(
        np.asarray(mesh.devices).reshape(8, 2, 4, 2, 2), ("inp", "xlo", "y", "xhi", "core")
    )
    out = ("xhi", "core")
    tok = P(out, wgt + ("inp",))
    up = P(wgt + out, "inp")
    down = P(("inp",) + out, wgt)
    return jax.shard_map(
        per_device,
        mesh=fine,
        in_specs=(tok, up, down, tok),
        out_specs=(tok, tok, up, down),
        check_vma=False,
    )
```

time: 206 us -> 201 us (0.976)
  waiting for transfers between devices: 117 us -> 114 us
    all_to_all x5, waiting for transfers between devices: 72.1 us -> 56.6 us  [exchange(): return lax.all_to_all(value, axis, 0, 0, tiled=True)]
    ppermute x10 -> x11, waiting for transfers between devices: 45.3 us -> 57.3 us  [swap(): return lax.ppermute(value, axis, pair)]
    unnamed x36 -> x24, local copies, waits for them, and re-layouts: 7.8 us -> 4.17 us
    convert_element_type x3 -> x4, other arithmetic: 7.28 us -> 5.44 us  [the longest x1 2.59 us: per_device(): (lax.optimization_barrier(near) + crossed.astype(f32)).astype(bf16)]
    pallas_call x8 -> x9, Pallas kernels: 22.8 us -> 24.6 us  [local(): pl.pallas_call(kernel, out_shape=[jax.ShapeDtypeStruct(shape, kind) for s...]
    ppermute x10 -> x11, starting transfers between devices: 15.9 us -> 15.4 us  [swap(): return lax.ppermute(value, axis, pair)]
  transfers between devices with their start and end apart: 15 -> 16, of which waited for: 8 -> 8; matrix products, arithmetic and copies ran while one was open for 7% -> 5% of each run, Pallas kernels for 9% -> 10%
where the time goes in v4:
time: 201 us; the launch traced here: 200 us
  waiting for transfers between devices  114 us (57%)
  starting transfers between devices  40.4 us (20%)
  Pallas kernels  24.6 us (12%)
  other arithmetic  12.9 us (6%)
  local copies, waits for them, and re-layouts  7.63 us (4%)
    ppermute x11, waiting for transfers between devices, swap(): return lax.ppermute(value, axis, pair)  57.3 us
    all_to_all x5, waiting for transfers between devices, exchange(): return lax.all_to_all(value, axis, 0, 0, tiled=True)  56.6 us
    all_to_all x5, starting transfers between devices, exchange(): return lax.all_to_all(value, axis, 0, 0, tiled=True)  25 us
    pallas_call x9, Pallas kernels, local(): pl.pallas_call(kernel, out_shape=[jax.ShapeDtypeStruct(shape, kind) for s...  24.6 us
    ppermute x11, starting transfers between devices, swap(): return lax.ppermute(value, axis, pair)  15.4 us
    unnamed x24, local copies, waits for them, and re-layouts  4.17 us
  transfers between devices with their start and end apart: 16, of which 8 were waited for; matrix products, arithmetic and copies ran while one was open for 5% of the time, Pallas kernels for 10%

profile of v4, /device:TPU:1, one launch (start us, length us, event | category | flops | bytes accessed | tf_op | source)
XLA Modules:
  0.0 200.3 jit_solution(8549883479683240094)
XLA Ops:
  0.6 3.7 %collective-permute-start.2 = (bf16[192,3072]{1,0:T(8,128)(2,1)}, bf16[192,3072]{1,0:T(8,128)(2,1)}, u32[]{:S(2)}, u32[]{:S(2)}) collective-permute-start(bf16[192,3072]{1,0:T(8,128)(2,1)} %w0.3), channel_id=1, source_target_pairs={{0,2},{2,0},{1,3},{3,1},{4,6},{6,4},{5,7},{7,5},{8,10},{10,8},{9,1... | collective-permute-start | bytes 3538952 | tf_op jit(solution)/shard_map/ppermute | solution.py:35
  4.3 0.8 pad_maximum_fusion.2
  5.1 0.9 broadcast_in_dim.4
  6.1 8.2 %all-to-all-start = ((bf16[8,192,256]{2,1,0:T(8,128)(2,1)}), bf16[8,192,256]{2,1,0:T(8,128)(2,1)S(1)}, u32[]{:S(2)}, u32[]{:S(2)}) async-start(bf16[8,192,256]{2,1,0:T(8,128)(2,1)} %broadcast_in_dim.4), calls=%async_computation | async-start | bytes 1572864 | tf_op jit(solution)/shard_map/all_to_all | solution.py:39
  14.2 1.3 collective-permute-start.1
  15.6 13.7 %collective-permute-done.2.w2 = bf16[192,3072]{1,0:T(8,128)(2,1)} collective-permute-done((bf16[192,3072]{1,0:T(8,128)(2,1)}, bf16[192,3072]{1,0:T(8,128)(2,1)}, u32[]{:S(2)}, u32[]{:S(2)}) %collective-permute-start.2) | collective-permute-done | bytes 1179680 | tf_op jit(solution)/shard_map/ppermute | solution.py:35
  29.2 2.3 %collective-permute-start.3 = (bf16[192,3072]{1,0:T(8,128)(2,1)}, bf16[192,3072]{1,0:T(8,128)(2,1)}, u32[]{:S(2)}, u32[]{:S(2)}) collective-permute-start(bf16[192,3072]{1,0:T(8,128)(2,1)} %collective-permute-done.2.w2), channel_id=1, source_target_pairs={{0,1},{1,0},{2,3},{3,2},{4,5},{5,4},{6,7},{7,6},{8,9},{9,8},{10,11... | collective-permute-start | bytes 3538952 | tf_op jit(solution)/shard_map/ppermute | solution.py:35
  31.5 0.1 pad_add_fusion.where
  31.6 6.2 %all-to-all-done.features = bf16[8,192,256]{2,1,0:T(8,128)(2,1)S(1)} async-done(((bf16[8,192,256]{2,1,0:T(8,128)(2,1)}), bf16[8,192,256]{2,1,0:T(8,128)(2,1)S(1)}, u32[]{:S(2)}, u32[]{:S(2)}) %all-to-all-start) | async-done | bytes 786464 | tf_op jit(solution)/shard_map/all_to_all | solution.py:39
  37.9 0.3 collective-permute-start.4
  38.2 5.6 %shard_map.75 = bf16[8,384,256]{2,1,0:T(8,128)(2,1)} custom-call(s32[4]{0:T(128)S(1)} %pad_add_fusion.where, bf16[8,192,256]{2,1,0:T(8,128)(2,1)S(1)} %all-to-all-done.features, bf16[192,3072]{1,0:T(8,128)(2,1)S(1)} %copy-done.10, bf16[192,3072]{1,0:T(8,128)(2,1)} %collective-permute-done.1.w1, bf16[192,3072]{1,0:T(8,128)(2,1)} %collective-permute-done.2.w2, ...), custom_call_target="tpu_custom_call" | custom-call | flops 4294967296 | bytes 65536 | tf_op jit(solution)/shard_map/pallas_call | solution.py:49
  43.8 5.8 %collective-permute-done.4.other = bf16[768,256]{1,0:T(8,128)(2,1)S(1)} collective-permute-done((bf16[768,256]{1,0:T(8,128)(2,1)S(1)}, bf16[768,256]{1,0:T(8,128)(2,1)S(1)}, u32[]{:S(2)}, u32[]{:S(2)}) %collective-permute-start.4) | collective-permute-done | bytes 393248 | tf_op jit(solution)/shard_map/ppermute | solution.py:35
  49.6 4.2 %all-to-all-start.1 = ((bf16[8,384,256]{2,1,0:T(8,128)(2,1)}), bf16[8,384,256]{2,1,0:T(8,128)(2,1)S(1)}, u32[]{:S(2)}, u32[]{:S(2)}) async-start(bf16[8,384,256]{2,1,0:T(8,128)(2,1)} %shard_map.75), calls=%async_computation.1 | async-start | bytes 3145728 | tf_op jit(solution)/shard_map/all_to_all | solution.py:39
  53.9 0.1 pad_add_fusion.1.where
  53.9 2.8 %maximum_select_fusion = bf16[2,768,768]{2,1,0:T(8,128)(2,1)S(1)} fusion(bf16[1,768,768]{2,1,0:T(8,128)(2,1)} %bitcast.7, bf16[1,768,768]{2,1,0:T(8,128)(2,1)} %bitcast.6, pred[]{:T(512)S(6)} %eq.3), kind=kLoop, calls=%fused_computation.1 | loop fusion | flops 3538944 | bytes 4718593 | tf_op jit(solution)/shard_map/jit(_where)/select_n | solution.py:43
  56.8 3.1 %shard_map.76 = bf16[2,8,192,256]{3,2,1,0:T(8,128)(2,1)} custom-call(s32[3]{0:T(128)S(1)} %pad_add_fusion.1.where, bf16[1536,768]{1,0:T(8,128)(2,1)S(1)} %bitcast.28, bf16[768,256]{1,0:T(8,128)(2,1)S(1)} %bitcast.31, bf16[768,256]{1,0:T(8,128)(2,1)S(1)} %collective-permute-done.4.other), custom_call_target="tpu_custom_call" | custom-call | flops 1048576 | bytes 65536 | tf_op jit(solution)/shard_map/pallas_call | solution.py:49
  59.8 1.4 copy-done
  61.3 13.1 %all-to-all-done.1.arrived = bf16[8,384,256]{2,1,0:T(8,128)(2,1)S(1)} async-done(((bf16[8,384,256]{2,1,0:T(8,128)(2,1)}), bf16[8,384,256]{2,1,0:T(8,128)(2,1)S(1)}, u32[]{:S(2)}, u32[]{:S(2)}) %all-to-all-start.1) | async-done | bytes 1572896 | tf_op jit(solution)/shard_map/all_to_all | solution.py:39
  74.4 4.4 %all-to-all-start.2 = ((bf16[16,192,256]{2,1,0:T(8,128)(2,1)}), bf16[16,192,256]{2,1,0:T(8,128)(2,1)}, u32[]{:S(2)}, u32[]{:S(2)}) async-start(bf16[16,192,256]{2,1,0:T(8,128)(2,1)} %bitcast.12), calls=%async_computation.2 | async-start | bytes 3145728 | tf_op jit(solution)/shard_map/all_to_all | solution.py:39
  78.8 1.0 shard_map.77
  79.8 2.9 %collective-permute-start.5 = (bf16[192,256]{1,0:T(8,128)(2,1)S(1)}, bf16[192,256]{1,0:T(8,128)(2,1)S(1)}, u32[]{:S(2)}, u32[]{:S(2)}) collective-permute-start(bf16[192,256]{1,0:T(8,128)(2,1)S(1)} %get-tuple-element.51), channel_id=1, source_target_pairs={{0,2},{2,0},{1,3},{3,1},{4,6},{6,4},{5,7},{7,5},{8,10},{10,8},{9,1... | collective-permute-start | bytes 294920 | tf_op jit(solution)/shard_map/ppermute | solution.py:35
  82.8 17.7 %collective-permute-done.5 = bf16[192,256]{1,0:T(8,128)(2,1)S(1)} collective-permute-done((bf16[192,256]{1,0:T(8,128)(2,1)S(1)}, bf16[192,256]{1,0:T(8,128)(2,1)S(1)}, u32[]{:S(2)}, u32[]{:S(2)}) %collective-permute-start.5) | collective-permute-done | bytes 98336 | tf_op jit(solution)/shard_map/ppermute | solution.py:35
  100.5 1.7 convert_reduce_fusion
  102.2 1.8 broadcast_in_dim.5
  104.1 4.2 %all-to-all-start.3 = ((bf16[8,768,256]{2,1,0:T(8,128)(2,1)}), bf16[8,768,256]{2,1,0:T(8,128)(2,1)S(1)}, u32[]{:S(2)}, u32[]{:S(2)}) async-start(bf16[8,768,256]{2,1,0:T(8,128)(2,1)} %broadcast_in_dim.5), calls=%async_computation.3 | async-start | bytes 6291456 | tf_op jit(solution)/shard_map/all_to_all | solution.py:39
  108.3 37.3 %all-to-all-done.3.gathered = bf16[8,768,256]{2,1,0:T(8,128)(2,1)S(1)} async-done(((bf16[8,768,256]{2,1,0:T(8,128)(2,1)}), bf16[8,768,256]{2,1,0:T(8,128)(2,1)S(1)}, u32[]{:S(2)}, u32[]{:S(2)}) %all-to-all-start.3) | async-done | bytes 3145760 | tf_op jit(solution)/shard_map/all_to_all | solution.py:39
  145.6 1.7 copy-done.1
  147.3 2.4 %shard_map.78 = (bf16[768,256]{1,0:T(8,128)(2,1)S(1)}, bf16[768,256]{1,0:T(8,128)(2,1)S(1)}) custom-call(s32[3]{0:T(128)S(1)} %pad_add_fusion.1.where, bf16[8,768,256]{2,1,0:T(8,128)(2,1)S(1)} %all-to-all-done.3.gathered, bf16[1536,768]{1,0:T(8,128)(2,1)S(1)} %bitcast.29), custom_call_target="tpu_custom_call" | custom-call | flops 1048576 | bytes 65536 | tf_op jit(solution)/shard_map/pallas_call | solution.py:49
  149.7 1.5 shard_map.79
  151.2 1.1 collective-permute-start.7
  152.4 0.1 pad_add_fusion.3.where
  152.4 3.4 %shard_map.80.given = bf16[8,192,256]{2,1,0:T(8,128)(2,1)S(1)} custom-call(s32[4]{0:T(128)S(1)} %pad_add_fusion.where, bf16[8,768,256]{2,1,0:T(8,128)(2,1)S(1)} %all-to-all-done.3.gathered, bf16[192,3072]{1,0:T(8,128)(2,1)S(1)} %copy-done.11, bf16[192,3072]{1,0:T(8,128)(2,1)} %collective-permute-done.1.w1, bf16[192,3072]{1,0:T(8,128)(2,1)} %collective-permute-done.2.w2, ...), custom_call_target="tpu_custom_call" | custom-call | flops 4294967296 | bytes 65536 | tf_op jit(solution)/shard_map/pallas_call | solution.py:49
  155.9 2.5 %shard_map.81 = (bf16[192,3072]{1,0:T(8,128)(2,1)}, bf16[192,3072]{1,0:T(8,128)(2,1)S(1)}) custom-call(s32[2]{0:T(128)S(1)} %pad_add_fusion.3.where, bf16[8,192,256]{2,1,0:T(8,128)(2,1)S(1)} %copy-done.3, bf16[8,768,256]{2,1,0:T(8,128)(2,1)S(1)} %all-to-all-done.3.gathered), custom_call_target="tpu_custom_call" | custom-call | flops 4294967296 | bytes 65536 | tf_op jit(solution)/shard_map/pallas_call | solution.py:49
  158.4 1.5 add_convert_fusion.2
  159.9 1.6 collective-permute-start.6
  161.4 3.5 %shard_map.83 = (bf16[768,768]{1,0:T(8,128)(2,1)}, bf16[768,768]{1,0:T(8,128)(2,1)S(1)}) custom-call(s32[3]{0:T(128)S(1)} %pad_add_fusion.1.where, bf16[8,768,256]{2,1,0:T(8,128)(2,1)S(1)} %all-to-all-done.3.gathered, bf16[768,256]{1,0:T(8,128)(2,1)S(1)} %bitcast.32, bf16[768,256]{1,0:T(8,128)(2,1)S(1)} %copy-done.9), custom_call_target="tpu_custom_call" | custom-call | flops 4294967296 | bytes 65536 | tf_op jit(solution)/shard_map/pallas_call | solution.py:49
  164.9 1.0 copy-done.4
  166.0 0.8 collective-permute-start.10
  166.8 1.4 collective-permute-start.9
  168.1 3.4 %collective-permute-done.6.other = bf16[768,256]{1,0:T(8,128)(2,1)S(1)} collective-permute-done((bf16[768,256]{1,0:T(8,128)(2,1)S(1)}, bf16[768,256]{1,0:T(8,128)(2,1)S(1)}, u32[]{:S(2)}, u32[]{:S(2)}) %collective-permute-start.6) | collective-permute-done | bytes 393248 | tf_op jit(solution)/shard_map/ppermute | solution.py:35
  171.6 1.6 shard_map.82
  173.1 4.0 %all-to-all-start.4 = ((bf16[8,192,256]{2,1,0:T(8,128)(2,1)}), bf16[8,192,256]{2,1,0:T(8,128)(2,1)S(1)}, u32[]{:S(2)}, u32[]{:S(2)}) async-start(bf16[8,192,256]{2,1,0:T(8,128)(2,1)} %shard_map.82), calls=%async_computation.4 | async-start | bytes 1572864 | tf_op jit(solution)/shard_map/all_to_all | solution.py:39
  177.2 1.8 convert_add_fusion
  178.9 1.3 add_convert_fusion
  180.3 16.7 %collective-permute-done.9 = bf16[192,3072]{1,0:T(8,128)(2,1)} collective-permute-done((bf16[192,3072]{1,0:T(8,128)(2,1)}, bf16[192,3072]{1,0:T(8,128)(2,1)}, u32[]{:S(2)}, u32[]{:S(2)}) %collective-permute-start.9) | collective-permute-done | bytes 1179680 | tf_op jit(solution)/shard_map/ppermute | solution.py:35
  197.0 2.6 %add_convert_fusion.1 = bf16[192,3072]{1,0:T(8,128)(2,1)} fusion(f32[192,3072]{1,0:T(8,128)S(1)} %convert_add_fusion, bf16[192,3072]{1,0:T(8,128)(2,1)} %collective-permute-done.9), kind=kLoop, calls=%fused_computation.3 | loop fusion | flops 1769472 | bytes 4718592 | tf_op jit(solution)/shard_map/convert_element_type | solution.py:211
  199.5 0.1 reduce_sum.25
  199.7 0.6 slice_bitcast_fusion
  (37 shorter events, 0.3 us)
Async XLA Ops:
  0.6 28.6 %collective-permute-start.2 = (bf16[192,3072]{1,0:T(8,128)(2,1)}, bf16[192,3072]{1,0:T(8,128)(2,1)}, u32[]{:S(2)}, u32[]{:S(2)}) collective-permute-start(bf16[192,3072]{1,0:T(8,128)(2,1)} %w0.3), channel_id=1, source_target_pairs={{0,2},{2,0},{1,3},{3,1},{4,6},{6,4},{5,7},{7,5},{8,10},{10,8},{9,1... | collective-permute-start | bytes 3538952 | tf_op jit(solution)/shard_map/ppermute | solution.py:35
  5.1 9.1 %copy-start.10 = (bf16[192,3072]{1,0:T(8,128)(2,1)S(1)}, bf16[192,3072]{1,0:T(8,128)(2,1)}, u32[]{:S(2)}) copy-start(bf16[192,3072]{1,0:T(8,128)(2,1)} %w0.3) | copy-start | bytes 3538948
  6.1 31.8 %all-to-all-start = ((bf16[8,192,256]{2,1,0:T(8,128)(2,1)}), bf16[8,192,256]{2,1,0:T(8,128)(2,1)S(1)}, u32[]{:S(2)}, u32[]{:S(2)}) async-start(bf16[8,192,256]{2,1,0:T(8,128)(2,1)} %broadcast_in_dim.4), calls=%async_computation | async-start | bytes 1572864 | tf_op jit(solution)/shard_map/all_to_all | solution.py:39
  14.2 23.9 %collective-permute-start.1 = (bf16[192,3072]{1,0:T(8,128)(2,1)S(1)}, bf16[192,3072]{1,0:T(8,128)(2,1)}, u32[]{:S(2)}, u32[]{:S(2)}) collective-permute-start(bf16[192,3072]{1,0:T(8,128)(2,1)S(1)} %copy-done.10), channel_id=1, source_target_pairs={{0,1},{1,0},{2,3},{3,2},{4,5},{5,4},{6,7},{7,6},{8,9},{9,8},{10,11... | collective-permute-start | bytes 3538952 | tf_op jit(solution)/shard_map/ppermute | solution.py:35
  29.2 8.9 %collective-permute-start.3 = (bf16[192,3072]{1,0:T(8,128)(2,1)}, bf16[192,3072]{1,0:T(8,128)(2,1)}, u32[]{:S(2)}, u32[]{:S(2)}) collective-permute-start(bf16[192,3072]{1,0:T(8,128)(2,1)} %collective-permute-done.2.w2), channel_id=1, source_target_pairs={{0,1},{1,0},{2,3},{3,2},{4,5},{5,4},{6,7},{7,6},{8,9},{9,8},{10,11... | collective-permute-start | bytes 3538952 | tf_op jit(solution)/shard_map/ppermute | solution.py:35
  31.5 22.4 %collective-permute-start = (bf16[768,768]{1,0:T(8,128)(2,1)}, bf16[768,768]{1,0:T(8,128)(2,1)}, u32[]{:S(2)}, u32[]{:S(2)}) collective-permute-start(bf16[768,768]{1,0:T(8,128)(2,1)} %param.6), channel_id=1, source_target_pairs={{0,1},{1,0},{2,3},{3,2},{4,5},{5,4},{6,7},{7,6},{8,9},{9,8},{10,11... | collective-permute-start | bytes 3538952 | tf_op jit(solution)/shard_map/ppermute | solution.py:35
  37.8 6.0 %copy-start.2 = (bf16[8,192,256]{2,1,0:T(8,128)(2,1)}, bf16[8,192,256]{2,1,0:T(8,128)(2,1)S(1)}, u32[]{:S(2)}) copy-start(bf16[8,192,256]{2,1,0:T(8,128)(2,1)S(1)} %all-to-all-done.features) | copy-start | bytes 2359300
  37.9 11.8 %collective-permute-start.4 = (bf16[768,256]{1,0:T(8,128)(2,1)S(1)}, bf16[768,256]{1,0:T(8,128)(2,1)S(1)}, u32[]{:S(2)}, u32[]{:S(2)}) collective-permute-start(bf16[768,256]{1,0:T(8,128)(2,1)S(1)} %bitcast.30), channel_id=1, source_target_pairs={{0,2},{2,0},{1,3},{3,1},{4,6},{6,4},{5,7},{7,5},{8,10},{10,8},{9,1... | collective-permute-start | bytes 1179656 | tf_op jit(solution)/shard_map/ppermute | solution.py:35
  49.6 7.1 %copy-start.8 = (bf16[768,256]{1,0:T(8,128)(2,1)}, bf16[768,256]{1,0:T(8,128)(2,1)S(1)}, u32[]{:S(2)}) copy-start(bf16[768,256]{1,0:T(8,128)(2,1)S(1)} %collective-permute-done.4.other) | copy-start | bytes 1179652
  49.6 24.7 %all-to-all-start.1 = ((bf16[8,384,256]{2,1,0:T(8,128)(2,1)}), bf16[8,384,256]{2,1,0:T(8,128)(2,1)S(1)}, u32[]{:S(2)}, u32[]{:S(2)}) async-start(bf16[8,384,256]{2,1,0:T(8,128)(2,1)} %shard_map.75), calls=%async_computation.1 | async-start | bytes 3145728 | tf_op jit(solution)/shard_map/all_to_all | solution.py:39
  59.8 1.4 copy-start
  74.4 26.1 %all-to-all-start.2 = ((bf16[16,192,256]{2,1,0:T(8,128)(2,1)}), bf16[16,192,256]{2,1,0:T(8,128)(2,1)}, u32[]{:S(2)}, u32[]{:S(2)}) async-start(bf16[16,192,256]{2,1,0:T(8,128)(2,1)} %bitcast.12), calls=%async_computation.2 | async-start | bytes 3145728 | tf_op jit(solution)/shard_map/all_to_all | solution.py:39
  79.8 20.6 %collective-permute-start.5 = (bf16[192,256]{1,0:T(8,128)(2,1)S(1)}, bf16[192,256]{1,0:T(8,128)(2,1)S(1)}, u32[]{:S(2)}, u32[]{:S(2)}) collective-permute-start(bf16[192,256]{1,0:T(8,128)(2,1)S(1)} %get-tuple-element.51), channel_id=1, source_target_pairs={{0,2},{2,0},{1,3},{3,1},{4,6},{6,4},{5,7},{7,5},{8,10},{10,8},{9,1... | collective-permute-start | bytes 294920 | tf_op jit(solution)/shard_map/ppermute | solution.py:35
  104.1 41.5 %all-to-all-start.3 = ((bf16[8,768,256]{2,1,0:T(8,128)(2,1)}), bf16[8,768,256]{2,1,0:T(8,128)(2,1)S(1)}, u32[]{:S(2)}, u32[]{:S(2)}) async-start(bf16[8,768,256]{2,1,0:T(8,128)(2,1)} %broadcast_in_dim.5), calls=%async_computation.3 | async-start | bytes 6291456 | tf_op jit(solution)/shard_map/all_to_all | solution.py:39
  145.6 1.7 copy-start.1
  147.3 2.4 %copy-start.3 = (bf16[8,192,256]{2,1,0:T(8,128)(2,1)S(1)}, bf16[8,192,256]{2,1,0:T(8,128)(2,1)}, u32[]{:S(2)}) copy-start(bf16[8,192,256]{2,1,0:T(8,128)(2,1)} %copy-done.2) | copy-start | bytes 2359300
  149.7 2.8 %copy-start.11 = (bf16[192,3072]{1,0:T(8,128)(2,1)S(1)}, bf16[192,3072]{1,0:T(8,128)(2,1)}, u32[]{:S(2)}) copy-start(bf16[192,3072]{1,0:T(8,128)(2,1)} %w0.3) | copy-start | bytes 3538948
  151.2 7.1 %collective-permute-start.7 = (bf16[192,3072]{1,0:T(8,128)(2,1)S(1)}, bf16[192,3072]{1,0:T(8,128)(2,1)S(1)}, u32[]{:S(2)}, u32[]{:S(2)}) collective-permute-start(bf16[192,3072]{1,0:T(8,128)(2,1)S(1)} %get-tuple-element.40), channel_id=1, source_target_pairs={{0,1},{1,0},{2,3},{3,2},{4,5},{5,4},{6,7},{7,6},{8,9},{9,8},{10,11... | collective-permute-start | bytes 3538952 | tf_op jit(solution)/shard_map/ppermute | solution.py:35
  158.4 1.5 copy-start.6
  158.4 3.1 %copy-start.9 = (bf16[768,256]{1,0:T(8,128)(2,1)S(1)}, bf16[768,256]{1,0:T(8,128)(2,1)}, u32[]{:S(2)}) copy-start(bf16[768,256]{1,0:T(8,128)(2,1)} %copy-done.8) | copy-start | bytes 1179652
  159.9 17.3 %collective-permute-start.8 = (bf16[192,3072]{1,0:T(8,128)(2,1)}, bf16[192,3072]{1,0:T(8,128)(2,1)}, u32[]{:S(2)}, u32[]{:S(2)}) collective-permute-start(bf16[192,3072]{1,0:T(8,128)(2,1)} %get-tuple-element.45), channel_id=1, source_target_pairs={{0,1},{1,0},{2,3},{3,2},{4,5},{5,4},{6,7},{7,6},{8,9},{9,8},{10,11... | collective-permute-start | bytes 3538952 | tf_op jit(solution)/shard_map/ppermute | solution.py:35
  159.9 11.7 %collective-permute-start.6 = (bf16[768,256]{1,0:T(8,128)(2,1)S(1)}, bf16[768,256]{1,0:T(8,128)(2,1)S(1)}, u32[]{:S(2)}, u32[]{:S(2)}) collective-permute-start(bf16[768,256]{1,0:T(8,128)(2,1)S(1)} %get-tuple-element.34), channel_id=1, source_target_pairs={{0,2},{2,0},{1,3},{3,1},{4,6},{6,4},{5,7},{7,5},{8,10},{10,8},{9,1... | collective-permute-start | bytes 1179656 | tf_op jit(solution)/shard_map/ppermute | solution.py:35
  164.9 1.0 copy-start.4
  166.0 12.9 %collective-permute-start.10 = (bf16[768,768]{1,0:T(8,128)(2,1)}, bf16[768,768]{1,0:T(8,128)(2,1)S(1)}, u32[]{:S(2)}, u32[]{:S(2)}) collective-permute-start(bf16[768,768]{1,0:T(8,128)(2,1)} %get-tuple-element.49), channel_id=1, source_target_pairs={{0,1},{1,0},{2,3},{3,2},{4,5},{5,4},{6,7},{7,6},{8,9},{9,8},{10,11... | collective-permute-start | bytes 3538952 | tf_op jit(solution)/shard_map/ppermute | solution.py:35
  166.8 30.2 %collective-permute-start.9 = (bf16[192,3072]{1,0:T(8,128)(2,1)}, bf16[192,3072]{1,0:T(8,128)(2,1)}, u32[]{:S(2)}, u32[]{:S(2)}) collective-permute-start(bf16[192,3072]{1,0:T(8,128)(2,1)} %add_convert_fusion.2), channel_id=1, source_target_pairs={{0,2},{2,0},{1,3},{3,1},{4,6},{6,4},{5,7},{7,5},{8,10},{10,8},{9,1... | collective-permute-start | bytes 3538952 | tf_op jit(solution)/shard_map/ppermute | solution.py:35
  173.1 4.0 %copy-start.7 = (bf16[192,3072]{1,0:T(8,128)(2,1)S(1)}, bf16[192,3072]{1,0:T(8,128)(2,1)}, u32[]{:S(2)}) copy-start(bf16[192,3072]{1,0:T(8,128)(2,1)} %copy-done.6) | copy-start | bytes 3538948
  173.1 26.4 %all-to-all-start.4 = ((bf16[8,192,256]{2,1,0:T(8,128)(2,1)}), bf16[8,192,256]{2,1,0:T(8,128)(2,1)S(1)}, u32[]{:S(2)}, u32[]{:S(2)}) async-start(bf16[8,192,256]{2,1,0:T(8,128)(2,1)} %shard_map.82), calls=%async_computation.4 | async-start | bytes 1572864 | tf_op jit(solution)/shard_map/all_to_all | solution.py:39
  177.1 1.8 copy-start.5

commit v5 on v4

--- a/solution.py
+++ b/solution.py
@@ -126,6 +126,10 @@
         total = dot(rows_of, rows, 1, 1).astype(bf16)
         sent[:, columns] = total[:192]
         kept[:, columns] = total[192:]
+
+
+def add_kernel(where, near, crossed, total):
+    total[...] = (near[...] + crossed[...].astype(f32)).astype(bf16)
 
 
 def tokens_kernel(where, gathered, w0, w1, w2, w3, payload):
@@ -208,7 +212,7 @@
     last = exchange(last, "inp")
     sums = jnp.sum(last.astype(f32), axis=0).astype(bf16)
     near = near_kept.astype(f32) + swap(near_sent, "core").astype(f32)
-    grad_up = (lax.optimization_barrier(near) + crossed.astype(f32)).astype(bf16)
+    (grad_up,) = local(add_kernel, [(192, 3072)], places, near, crossed)
     down_sent, down_kept = local(
         down_kernel, [(768, 768)] * 2, sides, gathered, g_own, g_other, flops=4 << 30
     )

time: 201 us -> 202 us (level)
  other arithmetic: 12.9 us -> 10.3 us
  Pallas kernels: 24.6 us -> 27.1 us
    convert_element_type x1 -> x0, other arithmetic: 2.59 us -> none  [per_device(): (lax.optimization_barrier(near) + crossed.astype(f32)).astype(bf16)]
    pallas_call x9 -> x10, Pallas kernels: 24.6 us -> 27.1 us  [local(): pl.pallas_call(kernel, out_shape=[jax.ShapeDtypeStruct(shape, kind) for s...]
  transfers between devices with their start and end apart: 16 -> 16, of which waited for: 8 -> 8; matrix products, arithmetic and copies ran while one was open for 5% -> 4% of each run, Pallas kernels for 10% -> 11%
where the time goes in v5:
time: 202 us
  waiting for transfers between devices  115 us (57%)
  starting transfers between devices  40.7 us (20%)
  Pallas kernels  27.1 us (13%)
  other arithmetic  10.3 us (5%)
  local copies, waits for them, and re-layouts  7.63 us (4%)
    ppermute x11, waiting for transfers between devices, swap(): return lax.ppermute(value, axis, pair)  58.5 us
    all_to_all x5, waiting for transfers between devices, exchange(): return lax.all_to_all(value, axis, 0, 0, tiled=True)  56.6 us
    pallas_call x10, Pallas kernels, local(): pl.pallas_call(kernel, out_shape=[jax.ShapeDtypeStruct(shape, kind) for s...  27.1 us
    all_to_all x5, starting transfers between devices, exchange(): return lax.all_to_all(value, axis, 0, 0, tiled=True)  25 us
    ppermute x11, starting transfers between devices, swap(): return lax.ppermute(value, axis, pair)  15.7 us
    unnamed x24, local copies, waits for them, and re-layouts  4.17 us
  transfers between devices with their start and end apart: 16, of which 8 were waited for; matrix products, arithmetic and copies ran while one was open for 4% of the time, Pallas kernels for 11%

profile of v5, /device:TPU:1, one launch (start us, length us, event | category | flops | bytes accessed | tf_op | source)
XLA Modules:
  0.0 201.5 jit_solution(7045749173830555392)
XLA Ops:
  0.6 3.7 %collective-permute-start.2 = (bf16[192,3072]{1,0:T(8,128)(2,1)}, bf16[192,3072]{1,0:T(8,128)(2,1)}, u32[]{:S(2)}, u32[]{:S(2)}) collective-permute-start(bf16[192,3072]{1,0:T(8,128)(2,1)} %w0.3), channel_id=1, source_target_pairs={{0,2},{2,0},{1,3},{3,1},{4,6},{6,4},{5,7},{7,5},{8,10},{10,8},{9,1... | collective-permute-start | bytes 3538952 | tf_op jit(solution)/shard_map/ppermute | solution.py:35
  4.3 0.8 pad_maximum_fusion.2
  5.1 0.9 broadcast_in_dim.4
  6.1 8.2 %all-to-all-start = ((bf16[8,192,256]{2,1,0:T(8,128)(2,1)}), bf16[8,192,256]{2,1,0:T(8,128)(2,1)S(1)}, u32[]{:S(2)}, u32[]{:S(2)}) async-start(bf16[8,192,256]{2,1,0:T(8,128)(2,1)} %broadcast_in_dim.4), calls=%async_computation | async-start | bytes 1572864 | tf_op jit(solution)/shard_map/all_to_all | solution.py:39
  14.2 1.3 collective-permute-start.1
  15.6 13.7 %collective-permute-done.2.w2 = bf16[192,3072]{1,0:T(8,128)(2,1)} collective-permute-done((bf16[192,3072]{1,0:T(8,128)(2,1)}, bf16[192,3072]{1,0:T(8,128)(2,1)}, u32[]{:S(2)}, u32[]{:S(2)}) %collective-permute-start.2) | collective-permute-done | bytes 1179680 | tf_op jit(solution)/shard_map/ppermute | solution.py:35
  29.2 2.3 %collective-permute-start.3 = (bf16[192,3072]{1,0:T(8,128)(2,1)}, bf16[192,3072]{1,0:T(8,128)(2,1)}, u32[]{:S(2)}, u32[]{:S(2)}) collective-permute-start(bf16[192,3072]{1,0:T(8,128)(2,1)} %collective-permute-done.2.w2), channel_id=1, source_target_pairs={{0,1},{1,0},{2,3},{3,2},{4,5},{5,4},{6,7},{7,6},{8,9},{9,8},{10,11... | collective-permute-start | bytes 3538952 | tf_op jit(solution)/shard_map/ppermute | solution.py:35
  31.5 0.1 pad_add_fusion.where
  31.6 6.2 %all-to-all-done.features = bf16[8,192,256]{2,1,0:T(8,128)(2,1)S(1)} async-done(((bf16[8,192,256]{2,1,0:T(8,128)(2,1)}), bf16[8,192,256]{2,1,0:T(8,128)(2,1)S(1)}, u32[]{:S(2)}, u32[]{:S(2)}) %all-to-all-start) | async-done | bytes 786464 | tf_op jit(solution)/shard_map/all_to_all | solution.py:39
  37.9 0.3 collective-permute-start.4
  38.2 5.6 %shard_map.75 = bf16[8,384,256]{2,1,0:T(8,128)(2,1)} custom-call(s32[4]{0:T(128)S(1)} %pad_add_fusion.where, bf16[8,192,256]{2,1,0:T(8,128)(2,1)S(1)} %all-to-all-done.features, bf16[192,3072]{1,0:T(8,128)(2,1)S(1)} %copy-done.10, bf16[192,3072]{1,0:T(8,128)(2,1)} %collective-permute-done.1.w1, bf16[192,3072]{1,0:T(8,128)(2,1)} %collective-permute-done.2.w2, ...), custom_call_target="tpu_custom_call" | custom-call | flops 4294967296 | bytes 65536 | tf_op jit(solution)/shard_map/pallas_call | solution.py:49
  43.8 5.8 %collective-permute-done.4.other = bf16[768,256]{1,0:T(8,128)(2,1)S(1)} collective-permute-done((bf16[768,256]{1,0:T(8,128)(2,1)S(1)}, bf16[768,256]{1,0:T(8,128)(2,1)S(1)}, u32[]{:S(2)}, u32[]{:S(2)}) %collective-permute-start.4) | collective-permute-done | bytes 393248 | tf_op jit(solution)/shard_map/ppermute | solution.py:35
  49.6 4.2 %all-to-all-start.1 = ((bf16[8,384,256]{2,1,0:T(8,128)(2,1)}), bf16[8,384,256]{2,1,0:T(8,128)(2,1)S(1)}, u32[]{:S(2)}, u32[]{:S(2)}) async-start(bf16[8,384,256]{2,1,0:T(8,128)(2,1)} %shard_map.75), calls=%async_computation.1 | async-start | bytes 3145728 | tf_op jit(solution)/shard_map/all_to_all | solution.py:39
  53.9 0.1 pad_add_fusion.1.where
  53.9 2.8 %maximum_select_fusion = bf16[2,768,768]{2,1,0:T(8,128)(2,1)S(1)} fusion(bf16[1,768,768]{2,1,0:T(8,128)(2,1)} %bitcast.7, bf16[1,768,768]{2,1,0:T(8,128)(2,1)} %bitcast.6, pred[]{:T(512)S(6)} %eq.3), kind=kLoop, calls=%fused_computation.1 | loop fusion | flops 3538944 | bytes 4718593 | tf_op jit(solution)/shard_map/jit(_where)/select_n | solution.py:43
  56.8 3.1 %shard_map.76 = bf16[2,8,192,256]{3,2,1,0:T(8,128)(2,1)} custom-call(s32[3]{0:T(128)S(1)} %pad_add_fusion.1.where, bf16[1536,768]{1,0:T(8,128)(2,1)S(1)} %bitcast.28, bf16[768,256]{1,0:T(8,128)(2,1)S(1)} %bitcast.31, bf16[768,256]{1,0:T(8,128)(2,1)S(1)} %collective-permute-done.4.other), custom_call_target="tpu_custom_call" | custom-call | flops 1048576 | bytes 65536 | tf_op jit(solution)/shard_map/pallas_call | solution.py:49
  59.8 1.4 copy-done
  61.3 13.1 %all-to-all-done.1.arrived = bf16[8,384,256]{2,1,0:T(8,128)(2,1)S(1)} async-done(((bf16[8,384,256]{2,1,0:T(8,128)(2,1)}), bf16[8,384,256]{2,1,0:T(8,128)(2,1)S(1)}, u32[]{:S(2)}, u32[]{:S(2)}) %all-to-all-start.1) | async-done | bytes 1572896 | tf_op jit(solution)/shard_map/all_to_all | solution.py:39
  74.4 4.4 %all-to-all-start.2 = ((bf16[16,192,256]{2,1,0:T(8,128)(2,1)}), bf16[16,192,256]{2,1,0:T(8,128)(2,1)}, u32[]{:S(2)}, u32[]{:S(2)}) async-start(bf16[16,192,256]{2,1,0:T(8,128)(2,1)} %bitcast.12), calls=%async_computation.2 | async-start | bytes 3145728 | tf_op jit(solution)/shard_map/all_to_all | solution.py:39
  78.8 1.0 shard_map.77
  79.8 2.9 %collective-permute-start.5 = (bf16[192,256]{1,0:T(8,128)(2,1)S(1)}, bf16[192,256]{1,0:T(8,128)(2,1)S(1)}, u32[]{:S(2)}, u32[]{:S(2)}) collective-permute-start(bf16[192,256]{1,0:T(8,128)(2,1)S(1)} %get-tuple-element.51), channel_id=1, source_target_pairs={{0,2},{2,0},{1,3},{3,1},{4,6},{6,4},{5,7},{7,5},{8,10},{10,8},{9,1... | collective-permute-start | bytes 294920 | tf_op jit(solution)/shard_map/ppermute | solution.py:35
  82.8 17.7 %collective-permute-done.5 = bf16[192,256]{1,0:T(8,128)(2,1)S(1)} collective-permute-done((bf16[192,256]{1,0:T(8,128)(2,1)S(1)}, bf16[192,256]{1,0:T(8,128)(2,1)S(1)}, u32[]{:S(2)}, u32[]{:S(2)}) %collective-permute-start.5) | collective-permute-done | bytes 98336 | tf_op jit(solution)/shard_map/ppermute | solution.py:35
  100.5 1.7 convert_reduce_fusion
  102.2 1.8 broadcast_in_dim.5
  104.1 4.2 %all-to-all-start.3 = ((bf16[8,768,256]{2,1,0:T(8,128)(2,1)}), bf16[8,768,256]{2,1,0:T(8,128)(2,1)S(1)}, u32[]{:S(2)}, u32[]{:S(2)}) async-start(bf16[8,768,256]{2,1,0:T(8,128)(2,1)} %broadcast_in_dim.5), calls=%async_computation.3 | async-start | bytes 6291456 | tf_op jit(solution)/shard_map/all_to_all | solution.py:39
  108.2 0.1 pad_add_fusion.2.where
  108.3 37.3 %all-to-all-done.3.gathered = bf16[8,768,256]{2,1,0:T(8,128)(2,1)S(1)} async-done(((bf16[8,768,256]{2,1,0:T(8,128)(2,1)}), bf16[8,768,256]{2,1,0:T(8,128)(2,1)S(1)}, u32[]{:S(2)}, u32[]{:S(2)}) %all-to-all-start.3) | async-done | bytes 3145760 | tf_op jit(solution)/shard_map/all_to_all | solution.py:39
  145.6 1.7 copy-done.1
  147.3 2.4 %shard_map.78 = (bf16[768,256]{1,0:T(8,128)(2,1)S(1)}, bf16[768,256]{1,0:T(8,128)(2,1)S(1)}) custom-call(s32[3]{0:T(128)S(1)} %pad_add_fusion.1.where, bf16[8,768,256]{2,1,0:T(8,128)(2,1)S(1)} %all-to-all-done.3.gathered, bf16[1536,768]{1,0:T(8,128)(2,1)S(1)} %bitcast.29), custom_call_target="tpu_custom_call" | custom-call | flops 1048576 | bytes 65536 | tf_op jit(solution)/shard_map/pallas_call | solution.py:49
  149.7 1.5 shard_map.79
  151.2 1.1 collective-permute-start.7
  152.4 3.4 %shard_map.80.given = bf16[8,192,256]{2,1,0:T(8,128)(2,1)S(1)} custom-call(s32[4]{0:T(128)S(1)} %pad_add_fusion.where, bf16[8,768,256]{2,1,0:T(8,128)(2,1)S(1)} %all-to-all-done.3.gathered, bf16[192,3072]{1,0:T(8,128)(2,1)S(1)} %copy-done.11, bf16[192,3072]{1,0:T(8,128)(2,1)} %collective-permute-done.1.w1, bf16[192,3072]{1,0:T(8,128)(2,1)} %collective-permute-done.2.w2, ...), custom_call_target="tpu_custom_call" | custom-call | flops 4294967296 | bytes 65536 | tf_op jit(solution)/shard_map/pallas_call | solution.py:49
  155.9 2.5 %shard_map.81 = (bf16[192,3072]{1,0:T(8,128)(2,1)}, bf16[192,3072]{1,0:T(8,128)(2,1)S(1)}) custom-call(s32[2]{0:T(128)S(1)} %pad_add_fusion.3.where, bf16[8,192,256]{2,1,0:T(8,128)(2,1)S(1)} %copy-done.3, bf16[8,768,256]{2,1,0:T(8,128)(2,1)S(1)} %all-to-all-done.3.gathered), custom_call_target="tpu_custom_call" | custom-call | flops 4294967296 | bytes 65536 | tf_op jit(solution)/shard_map/pallas_call | solution.py:49
  158.4 1.5 add_convert_fusion.1
  159.9 1.6 collective-permute-start.6
  161.4 1.4 collective-permute-start.9
  162.8 3.5 %shard_map.84 = (bf16[768,768]{1,0:T(8,128)(2,1)}, bf16[768,768]{1,0:T(8,128)(2,1)S(1)}) custom-call(s32[3]{0:T(128)S(1)} %pad_add_fusion.1.where, bf16[8,768,256]{2,1,0:T(8,128)(2,1)S(1)} %all-to-all-done.3.gathered, bf16[768,256]{1,0:T(8,128)(2,1)S(1)} %bitcast.32, bf16[768,256]{1,0:T(8,128)(2,1)S(1)} %copy-done.9), custom_call_target="tpu_custom_call" | custom-call | flops 4294967296 | bytes 65536 | tf_op jit(solution)/shard_map/pallas_call | solution.py:49
  166.3 1.0 copy-done.4
  167.4 1.1 collective-permute-start.10
  168.4 3.1 %collective-permute-done.6.other = bf16[768,256]{1,0:T(8,128)(2,1)S(1)} collective-permute-done((bf16[768,256]{1,0:T(8,128)(2,1)S(1)}, bf16[768,256]{1,0:T(8,128)(2,1)S(1)}, u32[]{:S(2)}, u32[]{:S(2)}) %collective-permute-start.6) | collective-permute-done | bytes 393248 | tf_op jit(solution)/shard_map/ppermute | solution.py:35
  171.6 1.5 shard_map.82
  173.1 4.0 %all-to-all-start.4 = ((bf16[8,192,256]{2,1,0:T(8,128)(2,1)}), bf16[8,192,256]{2,1,0:T(8,128)(2,1)S(1)}, u32[]{:S(2)}, u32[]{:S(2)}) async-start(bf16[8,192,256]{2,1,0:T(8,128)(2,1)} %shard_map.82), calls=%async_computation.4 | async-start | bytes 1572864 | tf_op jit(solution)/shard_map/all_to_all | solution.py:39
  177.2 1.7 convert_add_fusion.near
  178.8 18.1 %collective-permute-done.9.crossed = bf16[192,3072]{1,0:T(8,128)(2,1)} collective-permute-done((bf16[192,3072]{1,0:T(8,128)(2,1)}, bf16[192,3072]{1,0:T(8,128)(2,1)}, u32[]{:S(2)}, u32[]{:S(2)}) %collective-permute-start.9) | collective-permute-done | bytes 1179680 | tf_op jit(solution)/shard_map/ppermute | solution.py:35
  197.0 2.5 %shard_map.83 = bf16[192,3072]{1,0:T(8,128)(2,1)} custom-call(s32[4]{0:T(128)S(1)} %pad_add_fusion.where, f32[192,3072]{1,0:T(8,128)S(1)} %convert_add_fusion.near, bf16[192,3072]{1,0:T(8,128)(2,1)} %collective-permute-done.9.crossed), custom_call_target="tpu_custom_call" | custom-call | flops 1048576 | bytes 65536 | tf_op jit(solution)/shard_map/pallas_call | solution.py:49
  199.4 1.3 add_convert_fusion
  200.8 0.1 reduce_sum.25
  200.9 0.6 slice_bitcast_fusion
  (37 shorter events, 0.3 us)
Async XLA Ops:
  0.6 28.6 %collective-permute-start.2 = (bf16[192,3072]{1,0:T(8,128)(2,1)}, bf16[192,3072]{1,0:T(8,128)(2,1)}, u32[]{:S(2)}, u32[]{:S(2)}) collective-permute-start(bf16[192,3072]{1,0:T(8,128)(2,1)} %w0.3), channel_id=1, source_target_pairs={{0,2},{2,0},{1,3},{3,1},{4,6},{6,4},{5,7},{7,5},{8,10},{10,8},{9,1... | collective-permute-start | bytes 3538952 | tf_op jit(solution)/shard_map/ppermute | solution.py:35
  5.1 9.1 %copy-start.10 = (bf16[192,3072]{1,0:T(8,128)(2,1)S(1)}, bf16[192,3072]{1,0:T(8,128)(2,1)}, u32[]{:S(2)}) copy-start(bf16[192,3072]{1,0:T(8,128)(2,1)} %w0.3) | copy-start | bytes 3538948
  6.1 31.8 %all-to-all-start = ((bf16[8,192,256]{2,1,0:T(8,128)(2,1)}), bf16[8,192,256]{2,1,0:T(8,128)(2,1)S(1)}, u32[]{:S(2)}, u32[]{:S(2)}) async-start(bf16[8,192,256]{2,1,0:T(8,128)(2,1)} %broadcast_in_dim.4), calls=%async_computation | async-start | bytes 1572864 | tf_op jit(solution)/shard_map/all_to_all | solution.py:39
  14.2 23.9 %collective-permute-start.1 = (bf16[192,3072]{1,0:T(8,128)(2,1)S(1)}, bf16[192,3072]{1,0:T(8,128)(2,1)}, u32[]{:S(2)}, u32[]{:S(2)}) collective-permute-start(bf16[192,3072]{1,0:T(8,128)(2,1)S(1)} %copy-done.10), channel_id=1, source_target_pairs={{0,1},{1,0},{2,3},{3,2},{4,5},{5,4},{6,7},{7,6},{8,9},{9,8},{10,11... | collective-permute-start | bytes 3538952 | tf_op jit(solution)/shard_map/ppermute | solution.py:35
  29.2 8.9 %collective-permute-start.3 = (bf16[192,3072]{1,0:T(8,128)(2,1)}, bf16[192,3072]{1,0:T(8,128)(2,1)}, u32[]{:S(2)}, u32[]{:S(2)}) collective-permute-start(bf16[192,3072]{1,0:T(8,128)(2,1)} %collective-permute-done.2.w2), channel_id=1, source_target_pairs={{0,1},{1,0},{2,3},{3,2},{4,5},{5,4},{6,7},{7,6},{8,9},{9,8},{10,11... | collective-permute-start | bytes 3538952 | tf_op jit(solution)/shard_map/ppermute | solution.py:35
  31.5 22.4 %collective-permute-start = (bf16[768,768]{1,0:T(8,128)(2,1)}, bf16[768,768]{1,0:T(8,128)(2,1)}, u32[]{:S(2)}, u32[]{:S(2)}) collective-permute-start(bf16[768,768]{1,0:T(8,128)(2,1)} %param.6), channel_id=1, source_target_pairs={{0,1},{1,0},{2,3},{3,2},{4,5},{5,4},{6,7},{7,6},{8,9},{9,8},{10,11... | collective-permute-start | bytes 3538952 | tf_op jit(solution)/shard_map/ppermute | solution.py:35
  37.8 6.0 %copy-start.2 = (bf16[8,192,256]{2,1,0:T(8,128)(2,1)}, bf16[8,192,256]{2,1,0:T(8,128)(2,1)S(1)}, u32[]{:S(2)}) copy-start(bf16[8,192,256]{2,1,0:T(8,128)(2,1)S(1)} %all-to-all-done.features) | copy-start | bytes 2359300
  37.9 11.8 %collective-permute-start.4 = (bf16[768,256]{1,0:T(8,128)(2,1)S(1)}, bf16[768,256]{1,0:T(8,128)(2,1)S(1)}, u32[]{:S(2)}, u32[]{:S(2)}) collective-permute-start(bf16[768,256]{1,0:T(8,128)(2,1)S(1)} %bitcast.30), channel_id=1, source_target_pairs={{0,2},{2,0},{1,3},{3,1},{4,6},{6,4},{5,7},{7,5},{8,10},{10,8},{9,1... | collective-permute-start | bytes 1179656 | tf_op jit(solution)/shard_map/ppermute | solution.py:35
  49.6 7.1 %copy-start.8 = (bf16[768,256]{1,0:T(8,128)(2,1)}, bf16[768,256]{1,0:T(8,128)(2,1)S(1)}, u32[]{:S(2)}) copy-start(bf16[768,256]{1,0:T(8,128)(2,1)S(1)} %collective-permute-done.4.other) | copy-start | bytes 1179652
  49.6 24.7 %all-to-all-start.1 = ((bf16[8,384,256]{2,1,0:T(8,128)(2,1)}), bf16[8,384,256]{2,1,0:T(8,128)(2,1)S(1)}, u32[]{:S(2)}, u32[]{:S(2)}) async-start(bf16[8,384,256]{2,1,0:T(8,128)(2,1)} %shard_map.75), calls=%async_computation.1 | async-start | bytes 3145728 | tf_op jit(solution)/shard_map/all_to_all | solution.py:39
  59.8 1.4 copy-start
  74.4 26.1 %all-to-all-start.2 = ((bf16[16,192,256]{2,1,0:T(8,128)(2,1)}), bf16[16,192,256]{2,1,0:T(8,128)(2,1)}, u32[]{:S(2)}, u32[]{:S(2)}) async-start(bf16[16,192,256]{2,1,0:T(8,128)(2,1)} %bitcast.12), calls=%async_computation.2 | async-start | bytes 3145728 | tf_op jit(solution)/shard_map/all_to_all | solution.py:39
  79.8 20.6 %collective-permute-start.5 = (bf16[192,256]{1,0:T(8,128)(2,1)S(1)}, bf16[192,256]{1,0:T(8,128)(2,1)S(1)}, u32[]{:S(2)}, u32[]{:S(2)}) collective-permute-start(bf16[192,256]{1,0:T(8,128)(2,1)S(1)} %get-tuple-element.51), channel_id=1, source_target_pairs={{0,2},{2,0},{1,3},{3,1},{4,6},{6,4},{5,7},{7,5},{8,10},{10,8},{9,1... | collective-permute-start | bytes 294920 | tf_op jit(solution)/shard_map/ppermute | solution.py:35
  104.1 41.5 %all-to-all-start.3 = ((bf16[8,768,256]{2,1,0:T(8,128)(2,1)}), bf16[8,768,256]{2,1,0:T(8,128)(2,1)S(1)}, u32[]{:S(2)}, u32[]{:S(2)}) async-start(bf16[8,768,256]{2,1,0:T(8,128)(2,1)} %broadcast_in_dim.5), calls=%async_computation.3 | async-start | bytes 6291456 | tf_op jit(solution)/shard_map/all_to_all | solution.py:39
  145.6 1.7 copy-start.1
  147.3 2.4 %copy-start.3 = (bf16[8,192,256]{2,1,0:T(8,128)(2,1)S(1)}, bf16[8,192,256]{2,1,0:T(8,128)(2,1)}, u32[]{:S(2)}) copy-start(bf16[8,192,256]{2,1,0:T(8,128)(2,1)} %copy-done.2) | copy-start | bytes 2359300
  149.7 2.8 %copy-start.11 = (bf16[192,3072]{1,0:T(8,128)(2,1)S(1)}, bf16[192,3072]{1,0:T(8,128)(2,1)}, u32[]{:S(2)}) copy-start(bf16[192,3072]{1,0:T(8,128)(2,1)} %w0.3) | copy-start | bytes 3538948
  151.2 7.1 %collective-permute-start.7 = (bf16[192,3072]{1,0:T(8,128)(2,1)S(1)}, bf16[192,3072]{1,0:T(8,128)(2,1)S(1)}, u32[]{:S(2)}, u32[]{:S(2)}) collective-permute-start(bf16[192,3072]{1,0:T(8,128)(2,1)S(1)} %get-tuple-element.40), channel_id=1, source_target_pairs={{0,1},{1,0},{2,3},{3,2},{4,5},{5,4},{6,7},{7,6},{8,9},{9,8},{10,11... | collective-permute-start | bytes 3538952 | tf_op jit(solution)/shard_map/ppermute | solution.py:35
  158.4 1.5 copy-start.6
  158.4 4.5 %copy-start.9 = (bf16[768,256]{1,0:T(8,128)(2,1)S(1)}, bf16[768,256]{1,0:T(8,128)(2,1)}, u32[]{:S(2)}) copy-start(bf16[768,256]{1,0:T(8,128)(2,1)} %copy-done.8) | copy-start | bytes 1179652
  159.9 17.3 %collective-permute-start.8 = (bf16[192,3072]{1,0:T(8,128)(2,1)}, bf16[192,3072]{1,0:T(8,128)(2,1)}, u32[]{:S(2)}, u32[]{:S(2)}) collective-permute-start(bf16[192,3072]{1,0:T(8,128)(2,1)} %get-tuple-element.45), channel_id=1, source_target_pairs={{0,1},{1,0},{2,3},{3,2},{4,5},{5,4},{6,7},{7,6},{8,9},{9,8},{10,11... | collective-permute-start | bytes 3538952 | tf_op jit(solution)/shard_map/ppermute | solution.py:35
  159.9 11.7 %collective-permute-start.6 = (bf16[768,256]{1,0:T(8,128)(2,1)S(1)}, bf16[768,256]{1,0:T(8,128)(2,1)S(1)}, u32[]{:S(2)}, u32[]{:S(2)}) collective-permute-start(bf16[768,256]{1,0:T(8,128)(2,1)S(1)} %get-tuple-element.34), channel_id=1, source_target_pairs={{0,2},{2,0},{1,3},{3,1},{4,6},{6,4},{5,7},{7,5},{8,10},{10,8},{9,1... | collective-permute-start | bytes 1179656 | tf_op jit(solution)/shard_map/ppermute | solution.py:35
  161.4 35.5 %collective-permute-start.9 = (bf16[192,3072]{1,0:T(8,128)(2,1)}, bf16[192,3072]{1,0:T(8,128)(2,1)}, u32[]{:S(2)}, u32[]{:S(2)}) collective-permute-start(bf16[192,3072]{1,0:T(8,128)(2,1)} %add_convert_fusion.1), channel_id=1, source_target_pairs={{0,2},{2,0},{1,3},{3,1},{4,6},{6,4},{5,7},{7,5},{8,10},{10,8},{9,1... | collective-permute-start | bytes 3538952 | tf_op jit(solution)/shard_map/ppermute | solution.py:35
  166.3 1.0 copy-start.4
  167.4 32.1 %collective-permute-start.10 = (bf16[768,768]{1,0:T(8,128)(2,1)}, bf16[768,768]{1,0:T(8,128)(2,1)S(1)}, u32[]{:S(2)}, u32[]{:S(2)}) collective-permute-start(bf16[768,768]{1,0:T(8,128)(2,1)} %get-tuple-element.49), channel_id=1, source_target_pairs={{0,1},{1,0},{2,3},{3,2},{4,5},{5,4},{6,7},{7,6},{8,9},{9,8},{10,11... | collective-permute-start | bytes 3538952 | tf_op jit(solution)/shard_map/ppermute | solution.py:35
  173.1 4.0 %copy-start.7 = (bf16[192,3072]{1,0:T(8,128)(2,1)S(1)}, bf16[192,3072]{1,0:T(8,128)(2,1)}, u32[]{:S(2)}) copy-start(bf16[192,3072]{1,0:T(8,128)(2,1)} %copy-done.6) | copy-start | bytes 3538948
  173.1 27.7 %all-to-all-start.4 = ((bf16[8,192,256]{2,1,0:T(8,128)(2,1)}), bf16[8,192,256]{2,1,0:T(8,128)(2,1)S(1)}, u32[]{:S(2)}, u32[]{:S(2)}) async-start(bf16[8,192,256]{2,1,0:T(8,128)(2,1)} %shard_map.82), calls=%async_computation.4 | async-start | bytes 1572864 | tf_op jit(solution)/shard_map/all_to_all | solution.py:39
  178.8 20.6 %copy-start.5 = (bf16[768,768]{1,0:T(8,128)(2,1)S(1)}, bf16[768,768]{1,0:T(8,128)(2,1)}, u32[]{:S(2)}) copy-start(bf16[768,768]{1,0:T(8,128)(2,1)} %copy-done.4) | copy-start | bytes 3538948
